TPU v7x, 1024 devices: a whole 4x8x16 slice. The times are simulated.
1024 devices in a mesh: pipe: 8 (over y_lo, core), expert: 32 (over y_hi, z), dp: 4 (over x).
Axes of the slice: x: 4, y: 8 (y_hi: 2, y_lo: 4; y = y_hi * 4 + y_lo), z: 16, core: 2. Of those that a mesh axis runs over, the one named last changes fastest.
Arguments:
- stream: bfloat16 [8, 2, 2048, 7168], P('pipe', None, 'expert', 'dp'), may hold values from -11 to 11
- routes: int32 [8, 2, 2048, 8], P('pipe', None, 'expert'), may hold values from 0 to 255, as said below
- gates: float32 [8, 2, 2048, 8], P('pipe', None, 'expert'), may hold values from 0.2 to 1
- expert_hidden: bfloat16 [8, 2, 256, 16384], P('pipe', None, None, 'expert'), may hold values from -6 to 6
- down_weight: bfloat16 [8, 16384, 7168], P('pipe', 'expert', 'dp'), may hold values from -0.1875 to 0.1875
- norm_gain: float32 [8, 7168], P(None, 'dp'), may hold values from 0.5 to 1.5
Outputs:
- next_stream: bfloat16 [8, 2, 2048, 7168], P('pipe', None, 'expert', 'dp')
- next_normed: bfloat16 [8, 2, 2048, 7168], P('pipe', None, 'expert', 'dp')
Inputs may be any that keep to these rules, and one draw needn't show every extreme that they name: `routes`: each row names 8 different experts. For every expert below 16, at most 8 of the 64 rows of one aligned block of a micro-batch and section name it, and in each micro-batch of each section some expert below 16 is named by exactly 8 rows of every block.
All inputs are finite; a program needn't handle non-finite values.
Results may differ from a plain program's by a relative error of at most 0.0048.
Values may be sent and summed in bfloat16 or wider, within the bound.
No kernel may reach another device: no remote copies, remote signals or barrier semaphores. Data moves between devices by JAX's collectives and lax.ppermute only.
A program may use at most 32 MiB of HBM per device.

v0:
```python
import jax
import jax.numpy as jnp
from jax import lax
from jax.sharding import PartitionSpec as P

D = 7168


norm_epsilon = 1e-06


def passed_along(block, axis, distance):
    devices = range(lax.axis_size(axis))
    route = [(i - distance, i) for i in devices if i - distance in devices]
    return lax.ppermute(block, axis, route)


def route_weights(routes, gates, expert_count, capacity):
    owners = jnp.arange(expert_count, dtype=jnp.int32) // 2
    matches = routes[..., None] == owners
    is_routed = jnp.any(matches, axis=2)
    slot_rank = jnp.cumsum(is_routed.astype(jnp.int32), axis=1) - 1
    gate_sum = jnp.sum(jnp.where(matches, gates[..., None], 0.0), axis=2)
    positions = jnp.arange(capacity, dtype=jnp.int32)
    selected = is_routed[..., None] & (slot_rank[..., None] == positions)
    weights = jnp.where(selected, gate_sum[..., None], 0.0)
    return weights.reshape(weights.shape[0], weights.shape[1], expert_count * capacity)


def combine_rows(residual, received, weights):
    flat_rows = received.reshape(-1, received.shape[-1]).astype(jnp.float32)
    combined = jnp.einsum("tk,kd->td", weights, flat_rows, precision=lax.Precision.HIGHEST)
    return (residual.astype(jnp.float32) + combined).astype(jnp.bfloat16)


def normalize(rows, gain):
    floats = rows.astype(jnp.float32)
    totals = lax.psum(jnp.sum(floats * floats, axis=-1), "dp")
    factor = lax.rsqrt(totals / D + norm_epsilon)
    return (floats * factor[:, None] * gain).astype(jnp.bfloat16)


def section_gain(gain_table, section_index):
    picked = jnp.clip(section_index, 0, gain_table.shape[0] - 1)
    return lax.dynamic_index_in_dim(gain_table, picked, 0, keepdims=False)


def finish_block(layer_out, gain_table, batch_index):
    section_index = lax.axis_index("pipe")
    normed = normalize(layer_out, section_gain(gain_table, section_index))
    if batch_index == 0:
        moved = passed_along((layer_out, normed), "pipe", 1)
    else:
        moved = passed_along((layer_out, normed), "pipe", -1)
    return (moved[0], moved[1])


def per_device(stream, routes, gates, expert_hidden, down_weight, norm_gain):
    expert_count = lax.axis_size("expert")
    capacity = expert_hidden.shape[2] // expert_count
    feature_cols = stream.shape[3]
    outputs = jnp.einsum(
        "msf,fd->msd", expert_hidden[0], down_weight[0], preferred_element_type=jnp.float32
    )
    outputs = outputs.astype(jnp.bfloat16).reshape(2, expert_count, capacity, feature_cols)
    weights = route_weights(routes[0], gates[0], expert_count, capacity)
    results = []
    received = lax.all_to_all(outputs, "expert", split_axis=1, concat_axis=1, tiled=True)
    layers_out = [
        combine_rows(stream[0, batch_index], received[batch_index], weights[batch_index])
        for batch_index in range(2)
    ]
    for batch_index in range(2):
        results.append(finish_block(layers_out[batch_index], norm_gain, batch_index))
    next_stream = jnp.stack([results[0][0], results[1][0]], axis=0)[None]
    next_normed = jnp.stack([results[0][1], results[1][1]], axis=0)[None]
    return (next_stream, next_normed)


def solution(mesh):
    in_specs = (
        P("pipe", None, "expert", "dp"),
        P("pipe", None, "expert", None),
        P("pipe", None, "expert", None),
        P("pipe", None, None, "expert"),
        P("pipe", "expert", "dp"),
        P(None, "dp"),
    )
    out_specs = (P("pipe", None, "expert", "dp"), P("pipe", None, "expert", "dp"))
    return jax.shard_map(
        per_device, mesh=mesh, in_specs=in_specs, out_specs=out_specs, check_vma=False
    )
```

profile of v0, /device:TPU:72, one launch (start us, length us, event | category | flops | bytes accessed | tf_op | source)
XLA Modules:
  0.0 149.5 jit_solution(3667764523039266914)
XLA Ops:
  0.6 0.0 copy-start
  0.6 1.5 copy-done
  2.1 2.2 %fusion = bf16[2,32,8,1792]{3,2,1,0:T(8,128)(2,1)S(1)} fusion(bf16[1,512,1792]{2,1,0:T(8,128)(2,1)S(1)} %copy-done, bf16[1,2,256,512]{3,2,1,0:T(8,128)(2,1)} %param.9), kind=kOutput, calls=%fused_computation.1 | convolution fusion | flops 940441600 | bytes 4194304 | tf_op jit(solution)/shard_map/msf,fd->msd/dot_general | solution.py:62
  4.3 1.4 copy.22
  5.7 0.0 copy-start.2
  5.7 0.0 copy-start.3
  5.7 23.1 %all-to-all-start = ((bf16[2,32,8,1792]{3,2,0,1:T(8,128)(2,1)}), bf16[2,32,8,1792]{3,2,0,1:T(8,128)(2,1)}, u32[]{:S(2)}, u32[]{:S(2)}) async-start(bf16[2,32,8,1792]{3,2,0,1:T(8,128)(2,1)} %copy.22), calls=%async_computation | async-start | bytes 3670016 | tf_op jit(solution)/shard_map/all_to_all | solution.py:68
  28.8 0.0 copy-done.2
  28.8 0.1 compare_reduce_fusion
  28.9 0.1 copy.20
  29.0 0.1 reduce_window_sum.11
  29.1 0.1 copy.21
  29.2 0.9 dynamic-slice_reduce_fusion
  30.1 0.0 copy-done.3
  30.1 0.1 fusion.13
  30.2 0.0 copy-start.1
  30.2 91.0 %all-to-all-done = bf16[2,32,8,1792]{3,2,0,1:T(8,128)(2,1)} async-done(((bf16[2,32,8,1792]{3,2,0,1:T(8,128)(2,1)}), bf16[2,32,8,1792]{3,2,0,1:T(8,128)(2,1)}, u32[]{:S(2)}, u32[]{:S(2)}) %all-to-all-start) | async-done | bytes 1835040 | tf_op jit(solution)/shard_map/all_to_all | solution.py:68
  121.2 1.6 %fusion.16 = (bf16[1,32,8,1792]{3,2,0,1:T(8,128)(2,1)S(1)}, bf16[1,32,8,1792]{3,2,0,1:T(8,128)(2,1)S(1)}) fusion(bf16[2,32,8,1792]{3,2,0,1:T(8,128)(2,1)} %all-to-all-done), kind=kLoop, calls=%fused_computation.40 | loop fusion | bytes 3670016 | tf_op jit(solution)/shard_map/slice | solution.py:70
  122.8 0.0 copy-done.1
  122.8 0.8 fusion.10
  123.6 2.4 %collective-permute-start.1 = (bf16[64,1792]{1,0:T(8,128)(2,1)S(1)}, bf16[64,1792]{1,0:T(8,128)(2,1)S(1)}, u32[]{:S(2)}, u32[]{:S(2)}) collective-permute-start(bf16[64,1792]{1,0:T(8,128)(2,1)S(1)} %get-tuple-element.9), channel_id=1, source_target_pairs={{128,0},{256,128},{384,256},{512,384},{640,512},{768,640},{896,768... | collective-permute-start | bytes 688136 | tf_op jit(solution)/shard_map/ppermute | solution.py:15
  126.0 0.8 fusion.7
  126.8 1.9 %collective-permute-start = (bf16[64,1792]{1,0:T(8,128)(2,1)S(1)}, bf16[64,1792]{1,0:T(8,128)(2,1)S(1)}, u32[]{:S(2)}, u32[]{:S(2)}) collective-permute-start(bf16[64,1792]{1,0:T(8,128)(2,1)S(1)} %get-tuple-element.11), channel_id=1, source_target_pairs={{0,128},{128,256},{256,384},{384,512},{512,640},{640,768},{768,896... | collective-permute-start | bytes 688136 | tf_op jit(solution)/shard_map/ppermute | solution.py:15
  128.7 10.5 %all-reduce = (f32[64]{0:T(128)S(1)}, f32[64]{0:T(128)S(1)}) all-reduce(f32[64]{0:T(128)S(1)} %get-tuple-element.8, f32[64]{0:T(128)S(1)} %get-tuple-element.10), channel_id=1, replica_groups=mesh['pipe'=8,'expert'=32,'dp'=4] {'dp'}, use_global_device_ids=true, to_apply=%region_6.7 | all-reduce | flops 128 | bytes 1024 | tf_op jit(solution)/shard_map/psum | solution.py:38
  139.2 0.2 fusion.9
  139.4 1.9 %collective-permute-start.3 = (bf16[64,1792]{1,0:T(8,128)(2,1)S(1)}, bf16[64,1792]{1,0:T(8,128)(2,1)S(1)}, u32[]{:S(2)}, u32[]{:S(2)}) collective-permute-start(bf16[64,1792]{1,0:T(8,128)(2,1)S(1)} %get-tuple-element.7), channel_id=1, source_target_pairs={{128,0},{256,128},{384,256},{512,384},{640,512},{768,640},{896,768... | collective-permute-start | bytes 688136 | tf_op jit(solution)/shard_map/ppermute | solution.py:15
  141.3 2.4 %collective-permute-start.2 = (bf16[64,1792]{1,0:T(8,128)(2,1)S(1)}, bf16[64,1792]{1,0:T(8,128)(2,1)S(1)}, u32[]{:S(2)}, u32[]{:S(2)}) collective-permute-start(bf16[64,1792]{1,0:T(8,128)(2,1)S(1)} %get-tuple-element.6), channel_id=1, source_target_pairs={{0,128},{128,256},{256,384},{384,512},{512,640},{640,768},{768,896... | collective-permute-start | bytes 688136 | tf_op jit(solution)/shard_map/ppermute | solution.py:15
  143.8 0.0 collective-permute-done.1
  143.8 0.0 collective-permute-done
  143.8 0.8 maximum_bitcast_fusion
  144.6 0.3 collective-permute-done.3
  144.9 3.8 %collective-permute-done.2 = bf16[64,1792]{1,0:T(8,128)(2,1)S(1)} collective-permute-done((bf16[64,1792]{1,0:T(8,128)(2,1)S(1)}, bf16[64,1792]{1,0:T(8,128)(2,1)S(1)}, u32[]{:S(2)}, u32[]{:S(2)}) %collective-permute-start.2) | collective-permute-done | bytes 229408 | tf_op jit(solution)/shard_map/ppermute | solution.py:15
  148.7 0.8 maximum_bitcast_fusion.1
  (5 shorter events, 0.1 us)
Async XLA Ops:
  0.6 1.5 %copy-start = (bf16[1,512,1792]{2,1,0:T(8,128)(2,1)S(1)}, bf16[1,512,1792]{2,1,0:T(8,128)(2,1)}, u32[]{:S(2)}) copy-start(bf16[1,512,1792]{2,1,0:T(8,128)(2,1)} %param.10) | copy-start | bytes 5505028
  5.7 23.1 %copy-start.2 = (s32[1,2,64,8]{2,3,1,0:T(8,128)S(1)}, s32[1,2,64,8]{2,3,1,0:T(8,128)}, u32[]{:S(2)}) copy-start(s32[1,2,64,8]{2,3,1,0:T(8,128)} %param.7) | copy-start | bytes 12292
  5.7 24.4 %copy-start.3 = (f32[1,2,64,8]{2,3,1,0:T(8,128)S(1)}, f32[1,2,64,8]{2,3,1,0:T(8,128)}, u32[]{:S(2)}) copy-start(f32[1,2,64,8]{2,3,1,0:T(8,128)} %param.8) | copy-start | bytes 12292
  5.7 115.6 %all-to-all-start = ((bf16[2,32,8,1792]{3,2,0,1:T(8,128)(2,1)}), bf16[2,32,8,1792]{3,2,0,1:T(8,128)(2,1)}, u32[]{:S(2)}, u32[]{:S(2)}) async-start(bf16[2,32,8,1792]{3,2,0,1:T(8,128)(2,1)} %copy.22), calls=%async_computation | async-start | bytes 3670016 | tf_op jit(solution)/shard_map/all_to_all | solution.py:68
  30.2 92.6 %copy-start.1 = (bf16[1,2,64,1792]{3,2,1,0:T(8,128)(2,1)S(1)}, bf16[1,2,64,1792]{3,2,1,0:T(8,128)(2,1)}, u32[]{:S(2)}) copy-start(bf16[1,2,64,1792]{3,2,1,0:T(8,128)(2,1)} %param.6) | copy-start | bytes 1376260
  123.6 20.2 %collective-permute-start.1 = (bf16[64,1792]{1,0:T(8,128)(2,1)S(1)}, bf16[64,1792]{1,0:T(8,128)(2,1)S(1)}, u32[]{:S(2)}, u32[]{:S(2)}) collective-permute-start(bf16[64,1792]{1,0:T(8,128)(2,1)S(1)} %get-tuple-element.9), channel_id=1, source_target_pairs={{128,0},{256,128},{384,256},{512,384},{640,512},{768,640},{896,768... | collective-permute-start | bytes 688136 | tf_op jit(solution)/shard_map/ppermute | solution.py:15
  126.8 17.0 %collective-permute-start = (bf16[64,1792]{1,0:T(8,128)(2,1)S(1)}, bf16[64,1792]{1,0:T(8,128)(2,1)S(1)}, u32[]{:S(2)}, u32[]{:S(2)}) collective-permute-start(bf16[64,1792]{1,0:T(8,128)(2,1)S(1)} %get-tuple-element.11), channel_id=1, source_target_pairs={{0,128},{128,256},{256,384},{384,512},{512,640},{640,768},{768,896... | collective-permute-start | bytes 688136 | tf_op jit(solution)/shard_map/ppermute | solution.py:15
  139.4 5.4 %collective-permute-start.3 = (bf16[64,1792]{1,0:T(8,128)(2,1)S(1)}, bf16[64,1792]{1,0:T(8,128)(2,1)S(1)}, u32[]{:S(2)}, u32[]{:S(2)}) collective-permute-start(bf16[64,1792]{1,0:T(8,128)(2,1)S(1)} %get-tuple-element.7), channel_id=1, source_target_pairs={{128,0},{256,128},{384,256},{512,384},{640,512},{768,640},{896,768... | collective-permute-start | bytes 688136 | tf_op jit(solution)/shard_map/ppermute | solution.py:15
  141.3 7.3 %collective-permute-start.2 = (bf16[64,1792]{1,0:T(8,128)(2,1)S(1)}, bf16[64,1792]{1,0:T(8,128)(2,1)S(1)}, u32[]{:S(2)}, u32[]{:S(2)}) collective-permute-start(bf16[64,1792]{1,0:T(8,128)(2,1)S(1)} %get-tuple-element.6), channel_id=1, source_target_pairs={{0,128},{128,256},{256,384},{384,512},{512,640},{640,768},{768,896... | collective-permute-start | bytes 688136 | tf_op jit(solution)/shard_map/ppermute | solution.py:15
where the time goes:
time: 150 us; the launch traced here: 149 us
  waiting for transfers between devices  95.1 us (63%)
  starting transfers between devices  31.8 us (21%)
  blocking collectives  10.5 us (7%)
  local copies, waits for them, and re-layouts  5.45 us (4%)
  matrix products  3.69 us (2%)
  other arithmetic  2.18 us (1%)
    all_to_all x1, waiting for transfers between devices, per_device(): lax.all_to_all(outputs, 'expert', split_axis=1, concat_axis=1, tiled=True)  91 us
    all_to_all x1, starting transfers between devices, per_device(): lax.all_to_all(outputs, 'expert', split_axis=1, concat_axis=1, tiled=True)  23.1 us
    psum x1, blocking collectives, normalize(): totals = lax.psum(jnp.sum(floats * floats, axis=-1), 'dp')  10.5 us
    ppermute x4, starting transfers between devices, passed_along(): return lax.ppermute(block, axis, route)  8.65 us
    ppermute x4, waiting for transfers between devices, passed_along(): return lax.ppermute(block, axis, route)  4.1 us
  transfers between devices with their start and end apart: 5, of which 3 were waited for; matrix products, arithmetic and copies ran while one was open for 2% of the time, Pallas kernels for 0%

commit v1 on v0

v1 whole, which is shorter than its diff:
```python
import jax
import jax.numpy as jnp
from jax import lax
from jax.sharding import PartitionSpec as P

D = 7168
EPSILON = 1e-06
CAPACITY = 8


def shifted(block, distance):
    sections = range(lax.axis_size("pipe"))
    route = [(i - distance, i) for i in sections if i - distance in sections]
    return lax.ppermute(block, "pipe", route)


def shifted_to_partner(block, distance):
    sections, blocks = lax.axis_size("pipe"), lax.axis_size("expert")
    route = [
        (i * blocks + j, (i + distance) * blocks + (j ^ 1))
        for i in range(sections)
        if 0 <= i + distance < sections
        for j in range(blocks)
    ]
    return lax.ppermute(block, ("pipe", "expert"), route)


def route_weights(routes, gates, experts):
    matches = routes[:, :, None] == jnp.arange(experts, dtype=jnp.int32)
    is_routed = jnp.any(matches, axis=1)
    tokens = routes.shape[0]
    earlier = jnp.tril(jnp.ones((tokens, tokens), jnp.bfloat16), -1)
    rank = jnp.dot(earlier, is_routed.astype(jnp.bfloat16), preferred_element_type=jnp.float32)
    gate_sum = jnp.sum(jnp.where(matches, gates[:, :, None], 0.0), axis=1)
    slots = jnp.arange(CAPACITY, dtype=jnp.float32)
    chosen = is_routed[..., None] & (rank[..., None] == slots)
    return jnp.where(chosen, gate_sum[..., None], 0.0).reshape(tokens, experts * CAPACITY)


def per_device(stream, routes, gates, expert_hidden, down_weight, norm_gain):
    blocks = lax.axis_size("expert")
    experts = blocks // 2
    parity = lax.axis_index("expert") % 2
    section = lax.axis_index("pipe")
    sections = lax.axis_size("pipe")
    tokens, columns = stream.shape[2:]
    halves = [[j for j in range(blocks) if j % 2 == q] for q in range(2)]
    hidden = expert_hidden[0].reshape(2, experts, 2, CAPACITY, -1)
    kept = lax.dynamic_index_in_dim(hidden, parity, 2, keepdims=False).reshape(2, experts * CAPACITY, -1)
    sent = lax.dynamic_index_in_dim(hidden, 1 - parity, 2, keepdims=False).reshape(2, experts * CAPACITY, -1)

    def project(rows):
        return jnp.dot(rows, down_weight[0], preferred_element_type=jnp.float32).astype(jnp.bfloat16)

    sums = []
    for m, distance in enumerate((1, -1)):
        theirs = shifted_to_partner(project(sent[m]), distance)
        own = shifted(project(kept[m]), distance)
        total = (theirs.astype(jnp.float32) + own.astype(jnp.float32)).astype(jnp.bfloat16)
        sums.append(total.reshape(experts, CAPACITY, columns))
    exchanged = lax.all_to_all(
        jnp.stack(sums, axis=1), "expert", 0, 0, axis_index_groups=halves, tiled=True
    )
    outs = []
    for m, distance in enumerate((1, -1)):
        weights = route_weights(routes[0, m], gates[0, m], experts)
        high = weights.astype(jnp.bfloat16)
        low = (weights - high.astype(jnp.float32)).astype(jnp.bfloat16)
        side = shifted(jnp.concatenate([stream[0, m], high, low], axis=1), distance)
        received = exchanged[:, m].reshape(experts * CAPACITY, columns)
        residual = side[:, :columns].astype(jnp.float32)
        high, low = jnp.split(side[:, columns:], 2, axis=1)
        combined = jnp.dot(high, received, preferred_element_type=jnp.float32) + jnp.dot(
            low, received, preferred_element_type=jnp.float32
        )
        layer_out = (residual + combined).astype(jnp.bfloat16)
        floats = layer_out.astype(jnp.float32)
        totals = lax.psum(jnp.sum(floats * floats, axis=-1), "dp")
        gain = lax.dynamic_index_in_dim(norm_gain, jnp.clip(section - distance, 0, sections - 1), 0, keepdims=False)
        normed = (floats * lax.rsqrt(totals / D + EPSILON)[:, None] * gain).astype(jnp.bfloat16)
        outs.append((layer_out, normed))
    next_stream = jnp.stack([outs[0][0], outs[1][0]], axis=0)[None]
    next_normed = jnp.stack([outs[0][1], outs[1][1]], axis=0)[None]
    return (next_stream, next_normed)


def solution(mesh):
    in_specs = (
        P("pipe", None, "expert", "dp"),
        P("pipe", None, "expert", None),
        P("pipe", None, "expert", None),
        P("pipe", None, None, "expert"),
        P("pipe", "expert", "dp"),
        P(None, "dp"),
    )
    out_specs = (P("pipe", None, "expert", "dp"), P("pipe", None, "expert", "dp"))
    return jax.shard_map(
        per_device, mesh=mesh, in_specs=in_specs, out_specs=out_specs, check_vma=False
    )
```

time: 150 us -> 117 us (0.78)
  the two profiles are of different devices: /device:TPU:72 before, /device:TPU:200 now
where the time goes in v1:
time: 117 us; the launch traced here: 116 us
  waiting for transfers between devices  50.6 us (43%)
  starting transfers between devices  38.4 us (33%)
  blocking collectives  10.4 us (9%)
  matrix products  8.14 us (7%)
  other arithmetic  4.28 us (4%)
  local copies, waits for them, and re-layouts  3.12 us (3%)
    all_to_all x1, waiting for transfers between devices, per_device(): lax.all_to_all(jnp.stack(sums, axis=1), 'expert', 0, 0, axis_index_groups...  37.9 us
    all_to_all x1, starting transfers between devices, per_device(): lax.all_to_all(jnp.stack(sums, axis=1), 'expert', 0, 0, axis_index_groups...  21.1 us
    ppermute x4, starting transfers between devices, shifted(): return lax.ppermute(block, 'pipe', route)  11.6 us
    psum x1, blocking collectives, per_device(): totals = lax.psum(jnp.sum(floats * floats, axis=-1), 'dp')  10.4 us
    ppermute x2, waiting for transfers between devices, shifted_to_partner(): return lax.ppermute(block, ('pipe', 'expert'), route)  7.36 us
    ppermute x2, starting transfers between devices, shifted_to_partner(): return lax.ppermute(block, ('pipe', 'expert'), route)  5.7 us
    ppermute x4, waiting for transfers between devices, shifted(): return lax.ppermute(block, 'pipe', route)  5.34 us
    dot_general x4, matrix products, project(): jnp.dot(rows, down_weight[0], preferred_element_type=jnp.float32)  3.33 us
  transfers between devices with their start and end apart: 7, of which 5 were waited for; matrix products, arithmetic and copies ran while one was open for 6% of the time, Pallas kernels for 0%

profile of v1, /device:TPU:200, one launch (start us, length us, event | category | flops | bytes accessed | tf_op | source)
XLA Modules:
  0.0 115.9 jit_solution(16347552249216381208)
XLA Ops:
  0.6 0.0 copy-start
  0.6 0.0 copy-start.1
  0.7 1.5 %copy-done = bf16[1,512,1792]{2,1,0:T(8,128)(2,1)S(1)} copy-done((bf16[1,512,1792]{2,1,0:T(8,128)(2,1)S(1)}, bf16[1,512,1792]{2,1,0:T(8,128)(2,1)}, u32[]{:S(2)}) %copy-start) | copy-done | bytes 1835032
  2.1 1.3 %convolution_convert_fusion.3 = bf16[128,1792]{1,0:T(8,128)(2,1)S(1)} fusion(bf16[1,512,1792]{2,1,0:T(8,128)(2,1)S(1)} %copy-done, bf16[2,16,2,8,512]{4,3,2,1,0:T(8,128)(2,1)} %bitcast.84, s32[]{:T(128)S(6)} %select_n.44), kind=kOutput, calls=%fused_computation.3 | convolution fusion | flops 235110400 | bytes 2424836 | tf_op jit(solution)/shard_map/dot_general | solution.py:53
  3.5 1.9 %collective-permute-start.1 = (bf16[128,1792]{1,0:T(8,128)(2,1)S(1)}, bf16[128,1792]{1,0:T(8,128)(2,1)S(1)}, u32[]{:S(2)}, u32[]{:S(2)}) collective-permute-start(bf16[128,1792]{1,0:T(8,128)(2,1)S(1)} %convolution_convert_fusion.3), channel_id=1, source_target_pairs={{0,132},{4,128},{8,140},{12,136},{16,148},{20,144},{24,156},{28,15... | collective-permute-start | bytes 1376264 | tf_op jit(solution)/shard_map/ppermute | solution.py:25
  5.4 0.0 copy-done.1
  5.4 1.2 %convolution_convert_fusion.2 = bf16[128,1792]{1,0:T(8,128)(2,1)} fusion(bf16[1,512,1792]{2,1,0:T(8,128)(2,1)S(1)} %copy-done, bf16[2,16,2,8,512]{4,3,2,1,0:T(8,128)(2,1)S(1)} %bitcast.85, s32[]{:T(128)S(6)} %select_n.45), kind=kOutput, calls=%fused_computation.2 | convolution fusion | flops 235110400 | bytes 2424836 | tf_op jit(solution)/shard_map/dot_general | solution.py:53
  6.6 2.7 %collective-permute-start.2 = (bf16[128,1792]{1,0:T(8,128)(2,1)}, bf16[128,1792]{1,0:T(8,128)(2,1)}, u32[]{:S(2)}, u32[]{:S(2)}) collective-permute-start(bf16[128,1792]{1,0:T(8,128)(2,1)} %convolution_convert_fusion.2), channel_id=1, source_target_pairs={{0,128},{128,256},{256,384},{384,512},{512,640},{640,768},{768,896... | collective-permute-start | bytes 1376264 | tf_op jit(solution)/shard_map/ppermute | solution.py:14
  9.3 0.0 copy-start.3
  9.3 0.0 copy-start.4
  9.3 0.4 convolution_convert_fusion.1
  9.7 3.8 %collective-permute-start.3 = (bf16[128,1792]{1,0:T(8,128)(2,1)S(1)}, bf16[128,1792]{1,0:T(8,128)(2,1)S(1)}, u32[]{:S(2)}, u32[]{:S(2)}) collective-permute-start(bf16[128,1792]{1,0:T(8,128)(2,1)S(1)} %convolution_convert_fusion.1), channel_id=1, source_target_pairs={{128,4},{132,0},{136,12},{140,8},{144,20},{148,16},{152,28},{156,2... | collective-permute-start | bytes 1376264 | tf_op jit(solution)/shard_map/ppermute | solution.py:25
  13.5 0.4 convolution_convert_fusion
  13.9 3.3 %collective-permute-start.4 = (bf16[128,1792]{1,0:T(8,128)(2,1)S(1)}, bf16[128,1792]{1,0:T(8,128)(2,1)S(1)}, u32[]{:S(2)}, u32[]{:S(2)}) collective-permute-start(bf16[128,1792]{1,0:T(8,128)(2,1)S(1)} %convolution_convert_fusion), channel_id=1, source_target_pairs={{128,0},{256,128},{384,256},{512,384},{640,512},{768,640},{896,768... | collective-permute-start | bytes 1376264 | tf_op jit(solution)/shard_map/ppermute | solution.py:14
  17.2 0.0 copy-done.3
  17.3 0.0 copy-done.4
  17.3 0.9 collective-permute-done.1
  18.2 2.2 %collective-permute-done.2 = bf16[128,1792]{1,0:T(8,128)(2,1)} collective-permute-done((bf16[128,1792]{1,0:T(8,128)(2,1)}, bf16[128,1792]{1,0:T(8,128)(2,1)}, u32[]{:S(2)}, u32[]{:S(2)}) %collective-permute-start.2) | collective-permute-done | bytes 458784 | tf_op jit(solution)/shard_map/ppermute | solution.py:14
  20.4 1.1 fusion.10
  21.5 6.5 %collective-permute-done.3 = bf16[128,1792]{1,0:T(8,128)(2,1)S(1)} collective-permute-done((bf16[128,1792]{1,0:T(8,128)(2,1)S(1)}, bf16[128,1792]{1,0:T(8,128)(2,1)S(1)}, u32[]{:S(2)}, u32[]{:S(2)}) %collective-permute-start.3) | collective-permute-done | bytes 458784 | tf_op jit(solution)/shard_map/ppermute | solution.py:25
  28.0 0.0 collective-permute-done.4
  28.0 0.1 fusion.11
  28.1 1.0 pad_maximum_fusion
  29.1 0.0 copy-start.2
  29.1 21.1 %all-to-all-start = ((bf16[16,2,8,1792]{3,2,1,0:T(8,128)(2,1)}), bf16[16,2,8,1792]{3,2,1,0:T(8,128)(2,1)S(1)}, u32[]{:S(2)}, u32[]{:S(2)}) async-start(bf16[16,2,8,1792]{3,2,1,0:T(8,128)(2,1)} %pad_maximum_fusion), calls=%async_computation | async-start | bytes 1835008 | tf_op jit(solution)/shard_map/all_to_all | solution.py:61
  50.3 0.1 copy.38
  50.4 0.1 copy.43
  50.5 0.2 fusion.21
  50.7 0.1 copy.36
  50.7 0.2 fusion.19
  51.0 0.1 copy.41
  51.1 0.1 copy.37
  51.2 0.1 copy.42
  51.3 0.1 eq.79
  51.5 0.0 copy-done.2
  51.5 1.9 %collective-permute-start = (bf16[64,2048]{1,0:T(8,128)(2,1)S(1)}, bf16[64,2048]{1,0:T(8,128)(2,1)}, u32[]{:S(2)}, u32[]{:S(2)}) collective-permute-start(bf16[64,2048]{1,0:T(8,128)(2,1)S(1)} %pad_maximum_fusion.1), channel_id=1, source_target_pairs={{0,128},{128,256},{256,384},{384,512},{512,640},{640,768},{768,896... | collective-permute-start | bytes 786440 | tf_op jit(solution)/shard_map/ppermute | solution.py:14
  53.5 3.6 %collective-permute-start.5 = (bf16[64,2048]{1,0:T(8,128)(2,1)S(1)}, bf16[64,2048]{1,0:T(8,128)(2,1)}, u32[]{:S(2)}, u32[]{:S(2)}) collective-permute-start(bf16[64,2048]{1,0:T(8,128)(2,1)S(1)} %pad_maximum_fusion.2), channel_id=1, source_target_pairs={{128,0},{256,128},{384,256},{512,384},{640,512},{768,640},{896,768... | collective-permute-start | bytes 786440 | tf_op jit(solution)/shard_map/ppermute | solution.py:14
  57.2 0.9 dynamic-slice_reduce_fusion.1
  58.1 3.1 %collective-permute-done = bf16[64,2048]{1,0:T(8,128)(2,1)} collective-permute-done((bf16[64,2048]{1,0:T(8,128)(2,1)S(1)}, bf16[64,2048]{1,0:T(8,128)(2,1)}, u32[]{:S(2)}, u32[]{:S(2)}) %collective-permute-start) | collective-permute-done | bytes 262176 | tf_op jit(solution)/shard_map/ppermute | solution.py:14
  61.2 37.9 %all-to-all-done = bf16[16,2,8,1792]{3,2,1,0:T(8,128)(2,1)S(1)} async-done(((bf16[16,2,8,1792]{3,2,1,0:T(8,128)(2,1)}), bf16[16,2,8,1792]{3,2,1,0:T(8,128)(2,1)S(1)}, u32[]{:S(2)}, u32[]{:S(2)}) %all-to-all-start) | async-done | bytes 917536 | tf_op jit(solution)/shard_map/all_to_all | solution.py:61
  99.1 0.9 fusion.12
  100.0 1.3 %fusion.4 = (f32[64]{0:T(128)S(1)}, bf16[64,1792]{1,0:T(8,128)(2,1)S(1)}) fusion(f32[64,1792]{1,0:T(8,128)S(1)} %fusion.12, bf16[16,2,8,1792]{3,2,1,0:T(8,128)(2,1)S(1)} %all-to-all-done, bf16[64,2048]{1,0:T(8,128)(2,1)} %collective-permute-done), kind=kOutput, calls=%fused_computation.17 | convolution fusion | flops 30162880 | bytes 1392896 | tf_op jit(solution)/shard_map/dot_general | solution.py:73
  101.3 0.0 collective-permute-done.5
  101.4 0.9 fusion.13
  102.3 1.3 %fusion.7 = (f32[64]{0:T(128)S(1)}, bf16[64,1792]{1,0:T(8,128)(2,1)S(1)}) fusion(f32[64,1792]{1,0:T(8,128)S(1)} %fusion.13, bf16[16,2,8,1792]{3,2,1,0:T(8,128)(2,1)S(1)} %all-to-all-done, bf16[64,2048]{1,0:T(8,128)(2,1)} %collective-permute-done.5), kind=kOutput, calls=%fused_computation.20 | convolution fusion | flops 30162880 | bytes 1392896 | tf_op jit(solution)/shard_map/dot_general | solution.py:73
  103.6 10.4 %all-reduce = (f32[64]{0:T(128)S(1)}, f32[64]{0:T(128)S(1)}) all-reduce(f32[64]{0:T(128)S(1)} %get-tuple-element.16, f32[64]{0:T(128)S(1)} %get-tuple-element.18), channel_id=1, replica_groups=mesh['pipe'=8,'expert'=32,'dp'=4] {'dp'}, use_global_device_ids=true, to_apply=%region_7.8 | all-reduce | flops 128 | bytes 1024 | tf_op jit(solution)/shard_map/psum | solution.py:78
  114.0 0.1 fusion.15
  114.2 0.1 fusion.14
  114.3 0.8 maximum_bitcast_fusion.1
  115.1 0.8 maximum_bitcast_fusion
  (19 shorter events, 0.3 us)
Async XLA Ops:
  0.6 1.5 %copy-start = (bf16[1,512,1792]{2,1,0:T(8,128)(2,1)S(1)}, bf16[1,512,1792]{2,1,0:T(8,128)(2,1)}, u32[]{:S(2)}) copy-start(bf16[1,512,1792]{2,1,0:T(8,128)(2,1)} %param.10) | copy-start | bytes 5505028
  0.6 4.8 %copy-start.1 = (bf16[1,2,256,512]{3,2,1,0:T(8,128)(2,1)S(1)}, bf16[1,2,256,512]{3,2,1,0:T(8,128)(2,1)}, u32[]{:S(2)}) copy-start(bf16[1,2,256,512]{3,2,1,0:T(8,128)(2,1)} %param.9) | copy-start | bytes 1572868
  3.5 14.7 %collective-permute-start.1 = (bf16[128,1792]{1,0:T(8,128)(2,1)S(1)}, bf16[128,1792]{1,0:T(8,128)(2,1)S(1)}, u32[]{:S(2)}, u32[]{:S(2)}) collective-permute-start(bf16[128,1792]{1,0:T(8,128)(2,1)S(1)} %convolution_convert_fusion.3), channel_id=1, source_target_pairs={{0,132},{4,128},{8,140},{12,136},{16,148},{20,144},{24,156},{28,15... | collective-permute-start | bytes 1376264 | tf_op jit(solution)/shard_map/ppermute | solution.py:25
  6.6 13.8 %collective-permute-start.2 = (bf16[128,1792]{1,0:T(8,128)(2,1)}, bf16[128,1792]{1,0:T(8,128)(2,1)}, u32[]{:S(2)}, u32[]{:S(2)}) collective-permute-start(bf16[128,1792]{1,0:T(8,128)(2,1)} %convolution_convert_fusion.2), channel_id=1, source_target_pairs={{0,128},{128,256},{256,384},{384,512},{512,640},{640,768},{768,896... | collective-permute-start | bytes 1376264 | tf_op jit(solution)/shard_map/ppermute | solution.py:14
  9.3 8.0 %copy-start.3 = (s32[1,2,64,8]{2,3,1,0:T(8,128)S(1)}, s32[1,2,64,8]{2,3,1,0:T(8,128)}, u32[]{:S(2)}) copy-start(s32[1,2,64,8]{2,3,1,0:T(8,128)} %param.7) | copy-start | bytes 12292
  9.3 8.0 %copy-start.4 = (f32[1,2,64,8]{2,3,1,0:T(8,128)S(1)}, f32[1,2,64,8]{2,3,1,0:T(8,128)}, u32[]{:S(2)}) copy-start(f32[1,2,64,8]{2,3,1,0:T(8,128)} %param.8) | copy-start | bytes 12292
  9.7 18.3 %collective-permute-start.3 = (bf16[128,1792]{1,0:T(8,128)(2,1)S(1)}, bf16[128,1792]{1,0:T(8,128)(2,1)S(1)}, u32[]{:S(2)}, u32[]{:S(2)}) collective-permute-start(bf16[128,1792]{1,0:T(8,128)(2,1)S(1)} %convolution_convert_fusion.1), channel_id=1, source_target_pairs={{128,4},{132,0},{136,12},{140,8},{144,20},{148,16},{152,28},{156,2... | collective-permute-start | bytes 1376264 | tf_op jit(solution)/shard_map/ppermute | solution.py:25
  13.9 14.1 %collective-permute-start.4 = (bf16[128,1792]{1,0:T(8,128)(2,1)S(1)}, bf16[128,1792]{1,0:T(8,128)(2,1)S(1)}, u32[]{:S(2)}, u32[]{:S(2)}) collective-permute-start(bf16[128,1792]{1,0:T(8,128)(2,1)S(1)} %convolution_convert_fusion), channel_id=1, source_target_pairs={{128,0},{256,128},{384,256},{512,384},{640,512},{768,640},{896,768... | collective-permute-start | bytes 1376264 | tf_op jit(solution)/shard_map/ppermute | solution.py:14
  29.1 22.3 %copy-start.2 = (bf16[1,2,64,1792]{3,2,1,0:T(8,128)(2,1)S(1)}, bf16[1,2,64,1792]{3,2,1,0:T(8,128)(2,1)}, u32[]{:S(2)}) copy-start(bf16[1,2,64,1792]{3,2,1,0:T(8,128)(2,1)} %param.6) | copy-start | bytes 1376260
  29.1 70.0 %all-to-all-start = ((bf16[16,2,8,1792]{3,2,1,0:T(8,128)(2,1)}), bf16[16,2,8,1792]{3,2,1,0:T(8,128)(2,1)S(1)}, u32[]{:S(2)}, u32[]{:S(2)}) async-start(bf16[16,2,8,1792]{3,2,1,0:T(8,128)(2,1)} %pad_maximum_fusion), calls=%async_computation | async-start | bytes 1835008 | tf_op jit(solution)/shard_map/all_to_all | solution.py:61
  51.5 9.7 %collective-permute-start = (bf16[64,2048]{1,0:T(8,128)(2,1)S(1)}, bf16[64,2048]{1,0:T(8,128)(2,1)}, u32[]{:S(2)}, u32[]{:S(2)}) collective-permute-start(bf16[64,2048]{1,0:T(8,128)(2,1)S(1)} %pad_maximum_fusion.1), channel_id=1, source_target_pairs={{0,128},{128,256},{256,384},{384,512},{512,640},{640,768},{768,896... | collective-permute-start | bytes 786440 | tf_op jit(solution)/shard_map/ppermute | solution.py:14
  53.5 47.8 %collective-permute-start.5 = (bf16[64,2048]{1,0:T(8,128)(2,1)S(1)}, bf16[64,2048]{1,0:T(8,128)(2,1)}, u32[]{:S(2)}, u32[]{:S(2)}) collective-permute-start(bf16[64,2048]{1,0:T(8,128)(2,1)S(1)} %pad_maximum_fusion.2), channel_id=1, source_target_pairs={{128,0},{256,128},{384,256},{512,384},{640,512},{768,640},{896,768... | collective-permute-start | bytes 786440 | tf_op jit(solution)/shard_map/ppermute | solution.py:14

commit v2 on v1

--- a/solution.py
+++ b/solution.py
@@ -1,6 +1,8 @@
 import jax
 import jax.numpy as jnp
 from jax import lax
+from jax.experimental import pallas as pl
+from jax.experimental.pallas import tpu as pltpu
 from jax.sharding import PartitionSpec as P
 
 D = 7168
@@ -25,16 +27,46 @@
     return lax.ppermute(block, ("pipe", "expert"), route)
 
 
-def route_weights(routes, gates, experts):
-    matches = routes[:, :, None] == jnp.arange(experts, dtype=jnp.int32)
+def route_weights(routes, gates, experts, m):
+    tokens = routes.shape[0]
+    column = jnp.arange(experts * 2 * CAPACITY, dtype=jnp.int32)
+    matches = routes[:, :, None] == column // (2 * CAPACITY)
     is_routed = jnp.any(matches, axis=1)
-    tokens = routes.shape[0]
     earlier = jnp.tril(jnp.ones((tokens, tokens), jnp.bfloat16), -1)
     rank = jnp.dot(earlier, is_routed.astype(jnp.bfloat16), preferred_element_type=jnp.float32)
     gate_sum = jnp.sum(jnp.where(matches, gates[:, :, None], 0.0), axis=1)
-    slots = jnp.arange(CAPACITY, dtype=jnp.float32)
-    chosen = is_routed[..., None] & (rank[..., None] == slots)
-    return jnp.where(chosen, gate_sum[..., None], 0.0).reshape(tokens, experts * CAPACITY)
+    slot = column % (2 * CAPACITY) - m * CAPACITY
+    chosen = is_routed & (rank == slot.astype(jnp.float32)) & (slot >= 0)
+    return jnp.where(chosen, gate_sum, 0.0)
+
+
+def combine_kernel(received_ref, side0_ref, side1_ref, out_ref, squares_ref):
+    received = received_ref[...]
+    slots, columns = received.shape
+    for m, side_ref in enumerate((side0_ref, side1_ref)):
+        high = side_ref[:, columns : columns + slots]
+        low = side_ref[:, columns + slots :]
+        combined = jnp.dot(high, received, preferred_element_type=jnp.float32)
+        combined += jnp.dot(low, received, preferred_element_type=jnp.float32)
+        layer_out = (side_ref[:, :columns].astype(jnp.float32) + combined).astype(jnp.bfloat16)
+        out_ref[0, m] = layer_out
+        floats = layer_out.astype(jnp.float32)
+        squares_ref[m] = jnp.sum(floats * floats, axis=1, keepdims=True)
+
+
+def combine(received, sides, tokens):
+    slots, columns = received.shape
+    return pl.pallas_call(
+        combine_kernel,
+        out_shape=(
+            jax.ShapeDtypeStruct((1, 2, tokens, columns), jnp.bfloat16),
+            jax.ShapeDtypeStruct((2, tokens, 1), jnp.float32),
+        ),
+        cost_estimate=pl.CostEstimate(
+            flops=8 * tokens * slots * columns, bytes_accessed=2 * slots * columns, transcendentals=0
+        ),
+        compiler_params=pltpu.CompilerParams(vmem_limit_bytes=16 << 20),
+    )(received, *sides)
 
 
 def per_device(stream, routes, gates, expert_hidden, down_weight, norm_gain):
@@ -61,27 +93,23 @@
     exchanged = lax.all_to_all(
         jnp.stack(sums, axis=1), "expert", 0, 0, axis_index_groups=halves, tiled=True
     )
-    outs = []
+    sides = []
     for m, distance in enumerate((1, -1)):
-        weights = route_weights(routes[0, m], gates[0, m], experts)
+        weights = route_weights(routes[0, m], gates[0, m], experts, m)
         high = weights.astype(jnp.bfloat16)
         low = (weights - high.astype(jnp.float32)).astype(jnp.bfloat16)
-        side = shifted(jnp.concatenate([stream[0, m], high, low], axis=1), distance)
-        received = exchanged[:, m].reshape(experts * CAPACITY, columns)
-        residual = side[:, :columns].astype(jnp.float32)
-        high, low = jnp.split(side[:, columns:], 2, axis=1)
-        combined = jnp.dot(high, received, preferred_element_type=jnp.float32) + jnp.dot(
-            low, received, preferred_element_type=jnp.float32
-        )
-        layer_out = (residual + combined).astype(jnp.bfloat16)
-        floats = layer_out.astype(jnp.float32)
-        totals = lax.psum(jnp.sum(floats * floats, axis=-1), "dp")
-        gain = lax.dynamic_index_in_dim(norm_gain, jnp.clip(section - distance, 0, sections - 1), 0, keepdims=False)
-        normed = (floats * lax.rsqrt(totals / D + EPSILON)[:, None] * gain).astype(jnp.bfloat16)
-        outs.append((layer_out, normed))
-    next_stream = jnp.stack([outs[0][0], outs[1][0]], axis=0)[None]
-    next_normed = jnp.stack([outs[0][1], outs[1][1]], axis=0)[None]
-    return (next_stream, next_normed)
+        sides.append(shifted(jnp.concatenate([stream[0, m], high, low], axis=1), distance))
+    next_stream, squares = combine(exchanged.reshape(experts * 2 * CAPACITY, columns), sides, tokens)
+    totals = lax.psum(squares.reshape(2, tokens), "dp")
+    factor = lax.rsqrt(totals / D + EPSILON)
+    gains = jnp.stack(
+        [
+            lax.dynamic_index_in_dim(norm_gain, jnp.clip(section - distance, 0, sections - 1), 0, keepdims=False)
+            for distance in (1, -1)
+        ]
+    )
+    normed = next_stream.astype(jnp.float32) * factor[None, :, :, None] * gains[None, :, None, :]
+    return (next_stream, normed.astype(jnp.bfloat16))
 
 
 def solution(mesh):

time: 117 us -> 114 us (0.974)
  matrix products: 8.14 us -> 3.75 us
  other arithmetic: 4.28 us -> 6.62 us
  Pallas kernels: 0 us -> 1.52 us
    all_to_all x1, waiting for transfers between devices: 37.9 us -> 33.1 us  [per_device(): lax.all_to_all(jnp.stack(sums, axis=1), 'expert', 0, 0, axis_index_groups...]
    dot_general x4 -> x0, matrix products: 4.41 us -> none  [the longest x2 2.57 us: per_device(): jnp.dot(high, received, preferred_element_type=jnp.float32)]
    ppermute x4, waiting for transfers between devices: 5.34 us -> 9.27 us  [shifted(): return lax.ppermute(block, 'pipe', route)]
    convert_element_type x2, other arithmetic: 0.05 us -> 1.97 us  [the longest x1 1.97 us: per_device(): return (next_stream, normed.astype(jnp.bfloat16))]
    broadcast_in_dim x2 -> x0, other arithmetic: 1.62 us -> none  [the longest x1 0.81 us: per_device(): next_normed = jnp.stack([outs[0][1], outs[1][1]], axis=0)[None]]
    pallas_call x0 -> x1, Pallas kernels: none -> 1.52 us  [combine(): pl.pallas_call(combine_kernel, out_shape=(jax.ShapeDtypeStruct((1, 2, tok...]
    concatenate x2, other arithmetic: 0.04 us -> 1.47 us  [per_device(): jnp.concatenate([stream[0, m], high, low], axis=1)]
  transfers between devices with their start and end apart: 7 -> 7, of which waited for: 5 -> 6; matrix products, arithmetic and copies ran while one was open for 6% -> 6% of each run, Pallas kernels for 0% -> 0%
where the time goes in v2:
time: 114 us; the launch traced here: 113 us
  waiting for transfers between devices  49.8 us (44%)
  starting transfers between devices  37.3 us (33%)
  blocking collectives  10.5 us (9%)
  other arithmetic  6.62 us (6%)
  matrix products  3.75 us (3%)
  local copies, waits for them, and re-layouts  2.78 us (2%)
  Pallas kernels  1.52 us (1%)
    all_to_all x1, waiting for transfers between devices, per_device(): lax.all_to_all(jnp.stack(sums, axis=1), 'expert', 0, 0, axis_index_groups...  33.1 us
    all_to_all x1, starting transfers between devices, per_device(): lax.all_to_all(jnp.stack(sums, axis=1), 'expert', 0, 0, axis_index_groups...  21 us
    ppermute x4, starting transfers between devices, shifted(): return lax.ppermute(block, 'pipe', route)  10.7 us
    psum x1, blocking collectives, per_device(): totals = lax.psum(squares.reshape(2, tokens), 'dp')  10.5 us
    ppermute x4, waiting for transfers between devices, shifted(): return lax.ppermute(block, 'pipe', route)  9.27 us
    ppermute x2, waiting for transfers between devices, shifted_to_partner(): return lax.ppermute(block, ('pipe', 'expert'), route)  7.43 us
    ppermute x2, starting transfers between devices, shifted_to_partner(): return lax.ppermute(block, ('pipe', 'expert'), route)  5.7 us
    dot_general x4, matrix products, project(): jnp.dot(rows, down_weight[0], preferred_element_type=jnp.float32)  3.33 us
  transfers between devices with their start and end apart: 7, of which 6 were waited for; matrix products, arithmetic and copies ran while one was open for 6% of the time, Pallas kernels for 0%

profile of v2, /device:TPU:200, one launch (start us, length us, event | category | flops | bytes accessed | tf_op | source)
XLA Modules:
  0.0 113.1 jit_solution(9228856293535470170)
XLA Ops:
  0.6 0.0 copy-start
  0.6 0.0 copy-start.1
  0.7 1.5 %copy-done = bf16[1,512,1792]{2,1,0:T(8,128)(2,1)S(1)} copy-done((bf16[1,512,1792]{2,1,0:T(8,128)(2,1)S(1)}, bf16[1,512,1792]{2,1,0:T(8,128)(2,1)}, u32[]{:S(2)}) %copy-start) | copy-done | bytes 1835032
  2.1 1.3 %convolution_convert_fusion.3 = bf16[128,1792]{1,0:T(8,128)(2,1)S(1)} fusion(bf16[1,512,1792]{2,1,0:T(8,128)(2,1)S(1)} %copy-done, bf16[2,16,2,8,512]{4,3,2,1,0:T(8,128)(2,1)} %bitcast.46, s32[]{:T(128)S(6)} %select_n.78), kind=kOutput, calls=%fused_computation.3 | convolution fusion | flops 235110400 | bytes 2424836 | tf_op jit(solution)/shard_map/dot_general | solution.py:85
  3.5 1.9 %collective-permute-start = (bf16[128,1792]{1,0:T(8,128)(2,1)S(1)}, bf16[128,1792]{1,0:T(8,128)(2,1)S(1)}, u32[]{:S(2)}, u32[]{:S(2)}) collective-permute-start(bf16[128,1792]{1,0:T(8,128)(2,1)S(1)} %convolution_convert_fusion.3), channel_id=1, source_target_pairs={{0,132},{4,128},{8,140},{12,136},{16,148},{20,144},{24,156},{28,15... | collective-permute-start | bytes 1376264 | tf_op jit(solution)/shard_map/ppermute | solution.py:27
  5.4 0.0 copy-done.1
  5.4 1.2 %convolution_convert_fusion.2 = bf16[128,1792]{1,0:T(8,128)(2,1)} fusion(bf16[1,512,1792]{2,1,0:T(8,128)(2,1)S(1)} %copy-done, bf16[2,16,2,8,512]{4,3,2,1,0:T(8,128)(2,1)S(1)} %bitcast.47, s32[]{:T(128)S(6)} %select_n.79), kind=kOutput, calls=%fused_computation.2 | convolution fusion | flops 235110400 | bytes 2424836 | tf_op jit(solution)/shard_map/dot_general | solution.py:85
  6.6 2.7 %collective-permute-start.1 = (bf16[128,1792]{1,0:T(8,128)(2,1)}, bf16[128,1792]{1,0:T(8,128)(2,1)}, u32[]{:S(2)}, u32[]{:S(2)}) collective-permute-start(bf16[128,1792]{1,0:T(8,128)(2,1)} %convolution_convert_fusion.2), channel_id=1, source_target_pairs={{0,128},{128,256},{256,384},{384,512},{512,640},{640,768},{768,896... | collective-permute-start | bytes 1376264 | tf_op jit(solution)/shard_map/ppermute | solution.py:16
  9.3 0.4 convolution_convert_fusion.1
  9.7 3.8 %collective-permute-start.2 = (bf16[128,1792]{1,0:T(8,128)(2,1)S(1)}, bf16[128,1792]{1,0:T(8,128)(2,1)S(1)}, u32[]{:S(2)}, u32[]{:S(2)}) collective-permute-start(bf16[128,1792]{1,0:T(8,128)(2,1)S(1)} %convolution_convert_fusion.1), channel_id=1, source_target_pairs={{128,4},{132,0},{136,12},{140,8},{144,20},{148,16},{152,28},{156,2... | collective-permute-start | bytes 1376264 | tf_op jit(solution)/shard_map/ppermute | solution.py:27
  13.5 0.4 convolution_convert_fusion
  13.9 3.3 %collective-permute-start.3 = (bf16[128,1792]{1,0:T(8,128)(2,1)S(1)}, bf16[128,1792]{1,0:T(8,128)(2,1)S(1)}, u32[]{:S(2)}, u32[]{:S(2)}) collective-permute-start(bf16[128,1792]{1,0:T(8,128)(2,1)S(1)} %convolution_convert_fusion), channel_id=1, source_target_pairs={{128,0},{256,128},{384,256},{512,384},{640,512},{768,640},{896,768... | collective-permute-start | bytes 1376264 | tf_op jit(solution)/shard_map/ppermute | solution.py:16
  17.2 0.9 collective-permute-done
  18.2 2.2 %collective-permute-done.1 = bf16[128,1792]{1,0:T(8,128)(2,1)} collective-permute-done((bf16[128,1792]{1,0:T(8,128)(2,1)}, bf16[128,1792]{1,0:T(8,128)(2,1)}, u32[]{:S(2)}, u32[]{:S(2)}) %collective-permute-start.1) | collective-permute-done | bytes 458784 | tf_op jit(solution)/shard_map/ppermute | solution.py:16
  20.4 1.1 fusion.12
  21.5 6.5 %collective-permute-done.2 = bf16[128,1792]{1,0:T(8,128)(2,1)S(1)} collective-permute-done((bf16[128,1792]{1,0:T(8,128)(2,1)S(1)}, bf16[128,1792]{1,0:T(8,128)(2,1)S(1)}, u32[]{:S(2)}, u32[]{:S(2)}) %collective-permute-start.2) | collective-permute-done | bytes 458784 | tf_op jit(solution)/shard_map/ppermute | solution.py:27
  28.0 0.0 collective-permute-done.3
  28.0 0.1 fusion.13
  28.1 0.0 copy-start.3
  28.1 0.0 copy-start.4
  28.2 0.0 copy-start.2
  28.2 1.0 pad_maximum_fusion
  29.2 21.0 %all-to-all-start = ((bf16[16,2,8,1792]{3,2,1,0:T(8,128)(2,1)}), bf16[16,2,8,1792]{3,2,1,0:T(8,128)(2,1)S(1)}, u32[]{:S(2)}, u32[]{:S(2)}) async-start(bf16[16,2,8,1792]{3,2,1,0:T(8,128)(2,1)} %pad_maximum_fusion), calls=%async_computation | async-start | bytes 1835008 | tf_op jit(solution)/shard_map/all_to_all | solution.py:93
  50.2 0.0 copy-done.3
  50.2 0.1 copy.22
  50.3 0.1 copy.24
  50.4 0.0 copy-done.4
  50.4 0.1 copy.23
  50.5 0.1 copy.25
  50.6 0.4 compare_reduce_fusion
  51.0 0.4 fusion.11
  51.4 0.2 subtract_convert_fusion
  51.6 0.0 copy-done.2
  51.6 0.7 pad_maximum_fusion.2
  52.4 2.7 %collective-permute-start.5 = (bf16[64,2304]{1,0:T(8,128)(2,1)}, bf16[64,2304]{1,0:T(8,128)(2,1)S(1)}, u32[]{:S(2)}, u32[]{:S(2)}) collective-permute-start(bf16[64,2304]{1,0:T(8,128)(2,1)} %pad_maximum_fusion.2), channel_id=1, source_target_pairs={{128,0},{256,128},{384,256},{512,384},{640,512},{768,640},{896,768... | collective-permute-start | bytes 884744 | tf_op jit(solution)/shard_map/ppermute | solution.py:16
  55.1 0.2 subtract_convert_fusion.1
  55.3 0.7 pad_maximum_fusion.1
  56.1 1.9 %collective-permute-start.4 = (bf16[64,2304]{1,0:T(8,128)(2,1)}, bf16[64,2304]{1,0:T(8,128)(2,1)S(1)}, u32[]{:S(2)}, u32[]{:S(2)}) collective-permute-start(bf16[64,2304]{1,0:T(8,128)(2,1)} %pad_maximum_fusion.1), channel_id=1, source_target_pairs={{0,128},{128,256},{256,384},{384,512},{512,640},{640,768},{768,896... | collective-permute-start | bytes 884744 | tf_op jit(solution)/shard_map/ppermute | solution.py:16
  58.0 0.9 constant_dynamic-slice_fusion.1
  58.9 1.8 %collective-permute-done.5.side1_ref = bf16[64,2304]{1,0:T(8,128)(2,1)S(1)} collective-permute-done((bf16[64,2304]{1,0:T(8,128)(2,1)}, bf16[64,2304]{1,0:T(8,128)(2,1)S(1)}, u32[]{:S(2)}, u32[]{:S(2)}) %collective-permute-start.5) | collective-permute-done | bytes 294944 | tf_op jit(solution)/shard_map/ppermute | solution.py:16
  60.7 5.2 %collective-permute-done.4.side0_ref = bf16[64,2304]{1,0:T(8,128)(2,1)S(1)} collective-permute-done((bf16[64,2304]{1,0:T(8,128)(2,1)}, bf16[64,2304]{1,0:T(8,128)(2,1)S(1)}, u32[]{:S(2)}, u32[]{:S(2)}) %collective-permute-start.4) | collective-permute-done | bytes 294944 | tf_op jit(solution)/shard_map/ppermute | solution.py:16
  66.0 33.1 %all-to-all-done = bf16[16,2,8,1792]{3,2,1,0:T(8,128)(2,1)S(1)} async-done(((bf16[16,2,8,1792]{3,2,1,0:T(8,128)(2,1)}), bf16[16,2,8,1792]{3,2,1,0:T(8,128)(2,1)S(1)}, u32[]{:S(2)}, u32[]{:S(2)}) %all-to-all-start) | async-done | bytes 917536 | tf_op jit(solution)/shard_map/all_to_all | solution.py:93
  99.1 1.5 %shard_map.77 = (bf16[1,2,64,1792]{3,2,1,0:T(8,128)(2,1)}, f32[2,64,1]{2,1,0:T(8,128)S(1)}) custom-call(bf16[256,1792]{1,0:T(8,128)(2,1)S(1)} %bitcast.45, bf16[64,2304]{1,0:T(8,128)(2,1)S(1)} %collective-permute-done.4.side0_ref, bf16[64,2304]{1,0:T(8,128)(2,1)S(1)} %collective-permute-done.5.side1_ref), custom_call_target="tpu_custom_call" | custom-call | flops 234881024 | bytes 917504 | tf_op jit(solution)/shard_map/pallas_call | solution.py:59
  100.6 0.1 reduce
  100.7 10.5 %psum.7 = f32[2,64]{1,0:T(2,128)S(1)} all-reduce(f32[2,64]{1,0:T(2,128)S(1)} %reduce), channel_id=1, replica_groups=mesh['pipe'=8,'expert'=32,'dp'=4] {'dp'}, use_global_device_ids=true, to_apply=%region_4.5 | all-reduce | flops 128 | bytes 1024 | tf_op jit(solution)/shard_map/psum | solution.py:103
  111.2 2.0 %multiply_convert_fusion = bf16[1,2,64,1792]{3,2,1,0:T(8,128)(2,1)} fusion(bf16[1,2,64,1792]{3,2,1,0:T(8,128)(2,1)} %get-tuple-element.2, f32[2,1792]{1,0:T(2,128)S(1)} %pad_maximum_fusion.3, f32[2,64]{1,0:T(2,128)S(1)} %add_rsqrt_fusion), kind=kLoop, calls=%fused_computation.17 | loop fusion | flops 917504 | bytes 932352 | tf_op jit(solution)/shard_map/convert_element_type | solution.py:112
  (9 shorter events, 0.1 us)
Async XLA Ops:
  0.6 1.5 %copy-start = (bf16[1,512,1792]{2,1,0:T(8,128)(2,1)S(1)}, bf16[1,512,1792]{2,1,0:T(8,128)(2,1)}, u32[]{:S(2)}) copy-start(bf16[1,512,1792]{2,1,0:T(8,128)(2,1)} %param.10) | copy-start | bytes 5505028
  0.6 4.8 %copy-start.1 = (bf16[1,2,256,512]{3,2,1,0:T(8,128)(2,1)S(1)}, bf16[1,2,256,512]{3,2,1,0:T(8,128)(2,1)}, u32[]{:S(2)}) copy-start(bf16[1,2,256,512]{3,2,1,0:T(8,128)(2,1)} %param.9) | copy-start | bytes 1572868
  3.5 14.7 %collective-permute-start = (bf16[128,1792]{1,0:T(8,128)(2,1)S(1)}, bf16[128,1792]{1,0:T(8,128)(2,1)S(1)}, u32[]{:S(2)}, u32[]{:S(2)}) collective-permute-start(bf16[128,1792]{1,0:T(8,128)(2,1)S(1)} %convolution_convert_fusion.3), channel_id=1, source_target_pairs={{0,132},{4,128},{8,140},{12,136},{16,148},{20,144},{24,156},{28,15... | collective-permute-start | bytes 1376264 | tf_op jit(solution)/shard_map/ppermute | solution.py:27
  6.6 13.8 %collective-permute-start.1 = (bf16[128,1792]{1,0:T(8,128)(2,1)}, bf16[128,1792]{1,0:T(8,128)(2,1)}, u32[]{:S(2)}, u32[]{:S(2)}) collective-permute-start(bf16[128,1792]{1,0:T(8,128)(2,1)} %convolution_convert_fusion.2), channel_id=1, source_target_pairs={{0,128},{128,256},{256,384},{384,512},{512,640},{640,768},{768,896... | collective-permute-start | bytes 1376264 | tf_op jit(solution)/shard_map/ppermute | solution.py:16
  9.7 18.3 %collective-permute-start.2 = (bf16[128,1792]{1,0:T(8,128)(2,1)S(1)}, bf16[128,1792]{1,0:T(8,128)(2,1)S(1)}, u32[]{:S(2)}, u32[]{:S(2)}) collective-permute-start(bf16[128,1792]{1,0:T(8,128)(2,1)S(1)} %convolution_convert_fusion.1), channel_id=1, source_target_pairs={{128,4},{132,0},{136,12},{140,8},{144,20},{148,16},{152,28},{156,2... | collective-permute-start | bytes 1376264 | tf_op jit(solution)/shard_map/ppermute | solution.py:27
  13.9 14.1 %collective-permute-start.3 = (bf16[128,1792]{1,0:T(8,128)(2,1)S(1)}, bf16[128,1792]{1,0:T(8,128)(2,1)S(1)}, u32[]{:S(2)}, u32[]{:S(2)}) collective-permute-start(bf16[128,1792]{1,0:T(8,128)(2,1)S(1)} %convolution_convert_fusion), channel_id=1, source_target_pairs={{128,0},{256,128},{384,256},{512,384},{640,512},{768,640},{896,768... | collective-permute-start | bytes 1376264 | tf_op jit(solution)/shard_map/ppermute | solution.py:16
  28.1 22.0 %copy-start.3 = (s32[1,2,64,8]{2,3,1,0:T(8,128)S(1)}, s32[1,2,64,8]{2,3,1,0:T(8,128)}, u32[]{:S(2)}) copy-start(s32[1,2,64,8]{2,3,1,0:T(8,128)} %param.7) | copy-start | bytes 12292
  28.1 22.2 %copy-start.4 = (f32[1,2,64,8]{2,3,1,0:T(8,128)S(1)}, f32[1,2,64,8]{2,3,1,0:T(8,128)}, u32[]{:S(2)}) copy-start(f32[1,2,64,8]{2,3,1,0:T(8,128)} %param.8) | copy-start | bytes 12292
  28.2 23.4 %copy-start.2 = (bf16[1,2,64,1792]{3,2,1,0:T(8,128)(2,1)S(1)}, bf16[1,2,64,1792]{3,2,1,0:T(8,128)(2,1)}, u32[]{:S(2)}) copy-start(bf16[1,2,64,1792]{3,2,1,0:T(8,128)(2,1)} %param.6) | copy-start | bytes 1376260
  29.2 69.8 %all-to-all-start = ((bf16[16,2,8,1792]{3,2,1,0:T(8,128)(2,1)}), bf16[16,2,8,1792]{3,2,1,0:T(8,128)(2,1)S(1)}, u32[]{:S(2)}, u32[]{:S(2)}) async-start(bf16[16,2,8,1792]{3,2,1,0:T(8,128)(2,1)} %pad_maximum_fusion), calls=%async_computation | async-start | bytes 1835008 | tf_op jit(solution)/shard_map/all_to_all | solution.py:93
  52.4 8.4 %collective-permute-start.5 = (bf16[64,2304]{1,0:T(8,128)(2,1)}, bf16[64,2304]{1,0:T(8,128)(2,1)S(1)}, u32[]{:S(2)}, u32[]{:S(2)}) collective-permute-start(bf16[64,2304]{1,0:T(8,128)(2,1)} %pad_maximum_fusion.2), channel_id=1, source_target_pairs={{128,0},{256,128},{384,256},{512,384},{640,512},{768,640},{896,768... | collective-permute-start | bytes 884744 | tf_op jit(solution)/shard_map/ppermute | solution.py:16
  56.1 9.9 %collective-permute-start.4 = (bf16[64,2304]{1,0:T(8,128)(2,1)}, bf16[64,2304]{1,0:T(8,128)(2,1)S(1)}, u32[]{:S(2)}, u32[]{:S(2)}) collective-permute-start(bf16[64,2304]{1,0:T(8,128)(2,1)} %pad_maximum_fusion.1), channel_id=1, source_target_pairs={{0,128},{128,256},{256,384},{384,512},{512,640},{640,768},{768,896... | collective-permute-start | bytes 884744 | tf_op jit(solution)/shard_map/ppermute | solution.py:16

commit v3 on v2

--- a/solution.py
+++ b/solution.py
@@ -40,7 +40,11 @@
     return jnp.where(chosen, gate_sum, 0.0)
 
 
-def combine_kernel(received_ref, side0_ref, side1_ref, out_ref, squares_ref):
+def on_diagonal(size):
+    return lax.broadcasted_iota(jnp.int32, (size, size), 0) == lax.broadcasted_iota(jnp.int32, (size, size), 1)
+
+
+def combine_kernel(received_ref, side0_ref, side1_ref, out_ref, copy_ref, squares_ref):
     received = received_ref[...]
     slots, columns = received.shape
     for m, side_ref in enumerate((side0_ref, side1_ref)):
@@ -50,8 +54,10 @@
         combined += jnp.dot(low, received, preferred_element_type=jnp.float32)
         layer_out = (side_ref[:, :columns].astype(jnp.float32) + combined).astype(jnp.bfloat16)
         out_ref[0, m] = layer_out
+        copy_ref[m] = layer_out
         floats = layer_out.astype(jnp.float32)
-        squares_ref[m] = jnp.sum(floats * floats, axis=1, keepdims=True)
+        total = jnp.sum(floats * floats, axis=1, keepdims=True)
+        squares_ref[m : m + 1] = jnp.sum(jnp.where(on_diagonal(floats.shape[0]), total, 0.0), axis=0, keepdims=True)
 
 
 def combine(received, sides, tokens):
@@ -60,13 +66,33 @@
         combine_kernel,
         out_shape=(
             jax.ShapeDtypeStruct((1, 2, tokens, columns), jnp.bfloat16),
-            jax.ShapeDtypeStruct((2, tokens, 1), jnp.float32),
+            jax.ShapeDtypeStruct((2, tokens, columns), jnp.bfloat16),
+            jax.ShapeDtypeStruct((2, tokens), jnp.float32),
         ),
         cost_estimate=pl.CostEstimate(
             flops=8 * tokens * slots * columns, bytes_accessed=2 * slots * columns, transcendentals=0
         ),
-        compiler_params=pltpu.CompilerParams(vmem_limit_bytes=16 << 20),
+        compiler_params=pltpu.CompilerParams(vmem_limit_bytes=8 << 20),
     )(received, *sides)
+
+
+def norm_kernel(rows_ref, totals_ref, gains_ref, out_ref):
+    tokens, columns = rows_ref.shape[1:]
+    totals = jnp.sum(totals_ref[...], axis=0)
+    for m in range(2):
+        total = jnp.sum(jnp.where(on_diagonal(tokens), totals[m : m + 1], 0.0), axis=1, keepdims=True)
+        factor = lax.rsqrt(total / D + EPSILON)
+        normed = rows_ref[m].astype(jnp.float32) * factor * gains_ref[m : m + 1]
+        out_ref[0, m] = normed.astype(jnp.bfloat16)
+
+
+def normalize(rows, totals, gains):
+    return pl.pallas_call(
+        norm_kernel,
+        out_shape=jax.ShapeDtypeStruct((1, *rows.shape), jnp.bfloat16),
+        cost_estimate=pl.CostEstimate(flops=4 * rows.size, bytes_accessed=4 * rows.size, transcendentals=0),
+        compiler_params=pltpu.CompilerParams(vmem_limit_bytes=8 << 20),
+    )(rows, totals, gains)
 
 
 def per_device(stream, routes, gates, expert_hidden, down_weight, norm_gain):
@@ -99,17 +125,16 @@
         high = weights.astype(jnp.bfloat16)
         low = (weights - high.astype(jnp.float32)).astype(jnp.bfloat16)
         sides.append(shifted(jnp.concatenate([stream[0, m], high, low], axis=1), distance))
-    next_stream, squares = combine(exchanged.reshape(experts * 2 * CAPACITY, columns), sides, tokens)
-    totals = lax.psum(squares.reshape(2, tokens), "dp")
-    factor = lax.rsqrt(totals / D + EPSILON)
+    received = exchanged.reshape(experts * 2 * CAPACITY, columns)
+    next_stream, rows, squares = combine(received, sides, tokens)
+    totals = lax.all_gather(squares, "dp")
     gains = jnp.stack(
         [
             lax.dynamic_index_in_dim(norm_gain, jnp.clip(section - distance, 0, sections - 1), 0, keepdims=False)
             for distance in (1, -1)
         ]
     )
-    normed = next_stream.astype(jnp.float32) * factor[None, :, :, None] * gains[None, :, None, :]
-    return (next_stream, normed.astype(jnp.bfloat16))
+    return (next_stream, normalize(rows, totals, gains))
 
 
 def solution(mesh):

time: 114 us -> 112 us (0.982)
  other arithmetic: 6.62 us -> 4.52 us
    psum x1 -> x0, blocking collectives: 10.5 us -> none  [per_device(): totals = lax.psum(squares.reshape(2, tokens), 'dp')]
    all_gather x0 -> x1, blocking collectives: none -> 9.71 us  [per_device(): totals = lax.all_gather(squares, 'dp')]
    convert_element_type x1 -> x0, other arithmetic: 1.97 us -> none  [per_device(): return (next_stream, normed.astype(jnp.bfloat16))]
where the time goes in v3:
time: 112 us; the launch traced here: 111 us
  waiting for transfers between devices  49.8 us (44%)
  starting transfers between devices  37.3 us (33%)
  blocking collectives  9.71 us (9%)
  other arithmetic  4.52 us (4%)
  matrix products  3.75 us (3%)
  local copies, waits for them, and re-layouts  2.78 us (2%)
  Pallas kernels  2.49 us (2%)
    all_to_all x1, waiting for transfers between devices, per_device(): lax.all_to_all(jnp.stack(sums, axis=1), 'expert', 0, 0, axis_index_groups...  33.1 us
    all_to_all x1, starting transfers between devices, per_device(): lax.all_to_all(jnp.stack(sums, axis=1), 'expert', 0, 0, axis_index_groups...  21 us
    ppermute x4, starting transfers between devices, shifted(): return lax.ppermute(block, 'pipe', route)  10.7 us
    all_gather x1, blocking collectives, per_device(): totals = lax.all_gather(squares, 'dp')  9.71 us
    ppermute x4, waiting for transfers between devices, shifted(): return lax.ppermute(block, 'pipe', route)  9.27 us
    ppermute x2, waiting for transfers between devices, shifted_to_partner(): return lax.ppermute(block, ('pipe', 'expert'), route)  7.42 us
    ppermute x2, starting transfers between devices, shifted_to_partner(): return lax.ppermute(block, ('pipe', 'expert'), route)  5.7 us
    dot_general x4, matrix products, project(): jnp.dot(rows, down_weight[0], preferred_element_type=jnp.float32)  3.33 us
  transfers between devices with their start and end apart: 7, of which 6 were waited for; matrix products, arithmetic and copies ran while one was open for 6% of the time, Pallas kernels for 0%

profile of v3, /device:TPU:200, one launch (start us, length us, event | category | flops | bytes accessed | tf_op | source)
XLA Modules:
  0.0 111.2 jit_solution(13131468629997824424)
XLA Ops:
  0.6 0.0 copy-start
  0.6 0.0 copy-start.1
  0.7 1.5 %copy-done = bf16[1,512,1792]{2,1,0:T(8,128)(2,1)S(1)} copy-done((bf16[1,512,1792]{2,1,0:T(8,128)(2,1)S(1)}, bf16[1,512,1792]{2,1,0:T(8,128)(2,1)}, u32[]{:S(2)}) %copy-start) | copy-done | bytes 1835032
  2.1 1.3 %convolution_convert_fusion.3 = bf16[128,1792]{1,0:T(8,128)(2,1)S(1)} fusion(bf16[1,512,1792]{2,1,0:T(8,128)(2,1)S(1)} %copy-done, bf16[2,16,2,8,512]{4,3,2,1,0:T(8,128)(2,1)} %bitcast.48, s32[]{:T(128)S(6)} %select_n.78), kind=kOutput, calls=%fused_computation.3 | convolution fusion | flops 235110400 | bytes 2424836 | tf_op jit(solution)/shard_map/dot_general | solution.py:111
  3.5 1.9 %collective-permute-start = (bf16[128,1792]{1,0:T(8,128)(2,1)S(1)}, bf16[128,1792]{1,0:T(8,128)(2,1)S(1)}, u32[]{:S(2)}, u32[]{:S(2)}) collective-permute-start(bf16[128,1792]{1,0:T(8,128)(2,1)S(1)} %convolution_convert_fusion.3), channel_id=1, source_target_pairs={{0,132},{4,128},{8,140},{12,136},{16,148},{20,144},{24,156},{28,15... | collective-permute-start | bytes 1376264 | tf_op jit(solution)/shard_map/ppermute | solution.py:27
  5.4 0.0 copy-done.1
  5.4 1.2 %convolution_convert_fusion.2 = bf16[128,1792]{1,0:T(8,128)(2,1)} fusion(bf16[1,512,1792]{2,1,0:T(8,128)(2,1)S(1)} %copy-done, bf16[2,16,2,8,512]{4,3,2,1,0:T(8,128)(2,1)S(1)} %bitcast.49, s32[]{:T(128)S(6)} %select_n.79), kind=kOutput, calls=%fused_computation.2 | convolution fusion | flops 235110400 | bytes 2424836 | tf_op jit(solution)/shard_map/dot_general | solution.py:111
  6.6 2.7 %collective-permute-start.1 = (bf16[128,1792]{1,0:T(8,128)(2,1)}, bf16[128,1792]{1,0:T(8,128)(2,1)}, u32[]{:S(2)}, u32[]{:S(2)}) collective-permute-start(bf16[128,1792]{1,0:T(8,128)(2,1)} %convolution_convert_fusion.2), channel_id=1, source_target_pairs={{0,128},{128,256},{256,384},{384,512},{512,640},{640,768},{768,896... | collective-permute-start | bytes 1376264 | tf_op jit(solution)/shard_map/ppermute | solution.py:16
  9.3 0.4 convolution_convert_fusion.1
  9.7 3.8 %collective-permute-start.2 = (bf16[128,1792]{1,0:T(8,128)(2,1)S(1)}, bf16[128,1792]{1,0:T(8,128)(2,1)S(1)}, u32[]{:S(2)}, u32[]{:S(2)}) collective-permute-start(bf16[128,1792]{1,0:T(8,128)(2,1)S(1)} %convolution_convert_fusion.1), channel_id=1, source_target_pairs={{128,4},{132,0},{136,12},{140,8},{144,20},{148,16},{152,28},{156,2... | collective-permute-start | bytes 1376264 | tf_op jit(solution)/shard_map/ppermute | solution.py:27
  13.5 0.4 convolution_convert_fusion
  13.9 3.4 %collective-permute-start.3 = (bf16[128,1792]{1,0:T(8,128)(2,1)S(1)}, bf16[128,1792]{1,0:T(8,128)(2,1)S(1)}, u32[]{:S(2)}, u32[]{:S(2)}) collective-permute-start(bf16[128,1792]{1,0:T(8,128)(2,1)S(1)} %convolution_convert_fusion), channel_id=1, source_target_pairs={{128,0},{256,128},{384,256},{512,384},{640,512},{768,640},{896,768... | collective-permute-start | bytes 1376264 | tf_op jit(solution)/shard_map/ppermute | solution.py:16
  17.3 0.9 collective-permute-done
  18.2 2.2 %collective-permute-done.1 = bf16[128,1792]{1,0:T(8,128)(2,1)} collective-permute-done((bf16[128,1792]{1,0:T(8,128)(2,1)}, bf16[128,1792]{1,0:T(8,128)(2,1)}, u32[]{:S(2)}, u32[]{:S(2)}) %collective-permute-start.1) | collective-permute-done | bytes 458784 | tf_op jit(solution)/shard_map/ppermute | solution.py:16
  20.4 1.1 %fusion.12 = bf16[16,1,8,1792]{3,2,1,0:T(8,128)(2,1)S(1)} fusion(bf16[128,1792]{1,0:T(8,128)(2,1)} %collective-permute-done.1, bf16[128,1792]{1,0:T(8,128)(2,1)S(1)} %collective-permute-done), kind=kLoop, calls=%fused_computation.25 | loop fusion | flops 917504 | bytes 1376256 | tf_op jit(solution)/shard_map/stack;reshape | solution.py:120
  21.5 6.5 %collective-permute-done.2 = bf16[128,1792]{1,0:T(8,128)(2,1)S(1)} collective-permute-done((bf16[128,1792]{1,0:T(8,128)(2,1)S(1)}, bf16[128,1792]{1,0:T(8,128)(2,1)S(1)}, u32[]{:S(2)}, u32[]{:S(2)}) %collective-permute-start.2) | collective-permute-done | bytes 458784 | tf_op jit(solution)/shard_map/ppermute | solution.py:27
  28.0 0.0 collective-permute-done.3
  28.0 0.1 fusion.13
  28.1 0.0 copy-start.3
  28.1 0.0 copy-start.4
  28.2 0.0 copy-start.2
  28.2 1.0 pad_maximum_fusion
  29.2 21.0 %all-to-all-start = ((bf16[16,2,8,1792]{3,2,1,0:T(8,128)(2,1)}), bf16[16,2,8,1792]{3,2,1,0:T(8,128)(2,1)S(1)}, u32[]{:S(2)}, u32[]{:S(2)}) async-start(bf16[16,2,8,1792]{3,2,1,0:T(8,128)(2,1)} %pad_maximum_fusion), calls=%async_computation | async-start | bytes 1835008 | tf_op jit(solution)/shard_map/all_to_all | solution.py:119
  50.1 0.0 copy-done.3
  50.2 0.1 copy.22
  50.2 0.1 copy.24
  50.3 0.0 copy-done.4
  50.3 0.1 copy.23
  50.4 0.1 copy.25
  50.5 0.4 compare_reduce_fusion
  50.9 0.4 fusion.11
  51.3 0.2 subtract_convert_fusion
  51.5 0.0 copy-done.2
  51.6 0.7 pad_maximum_fusion.2
  52.3 2.7 %collective-permute-start.5 = (bf16[64,2304]{1,0:T(8,128)(2,1)}, bf16[64,2304]{1,0:T(8,128)(2,1)S(1)}, u32[]{:S(2)}, u32[]{:S(2)}) collective-permute-start(bf16[64,2304]{1,0:T(8,128)(2,1)} %pad_maximum_fusion.2), channel_id=1, source_target_pairs={{128,0},{256,128},{384,256},{512,384},{640,512},{768,640},{896,768... | collective-permute-start | bytes 884744 | tf_op jit(solution)/shard_map/ppermute | solution.py:16
  55.1 0.2 subtract_convert_fusion.1
  55.3 0.7 pad_maximum_fusion.1
  56.0 1.9 %collective-permute-start.4 = (bf16[64,2304]{1,0:T(8,128)(2,1)}, bf16[64,2304]{1,0:T(8,128)(2,1)S(1)}, u32[]{:S(2)}, u32[]{:S(2)}) collective-permute-start(bf16[64,2304]{1,0:T(8,128)(2,1)} %pad_maximum_fusion.1), channel_id=1, source_target_pairs={{0,128},{128,256},{256,384},{384,512},{512,640},{640,768},{768,896... | collective-permute-start | bytes 884744 | tf_op jit(solution)/shard_map/ppermute | solution.py:16
  58.0 0.9 constant_dynamic-slice_fusion.1
  58.9 1.8 %collective-permute-done.5.side1_ref = bf16[64,2304]{1,0:T(8,128)(2,1)S(1)} collective-permute-done((bf16[64,2304]{1,0:T(8,128)(2,1)}, bf16[64,2304]{1,0:T(8,128)(2,1)S(1)}, u32[]{:S(2)}, u32[]{:S(2)}) %collective-permute-start.5) | collective-permute-done | bytes 294944 | tf_op jit(solution)/shard_map/ppermute | solution.py:16
  60.7 5.2 %collective-permute-done.4.side0_ref = bf16[64,2304]{1,0:T(8,128)(2,1)S(1)} collective-permute-done((bf16[64,2304]{1,0:T(8,128)(2,1)}, bf16[64,2304]{1,0:T(8,128)(2,1)S(1)}, u32[]{:S(2)}, u32[]{:S(2)}) %collective-permute-start.4) | collective-permute-done | bytes 294944 | tf_op jit(solution)/shard_map/ppermute | solution.py:16
  66.0 33.1 %all-to-all-done = bf16[16,2,8,1792]{3,2,1,0:T(8,128)(2,1)S(1)} async-done(((bf16[16,2,8,1792]{3,2,1,0:T(8,128)(2,1)}), bf16[16,2,8,1792]{3,2,1,0:T(8,128)(2,1)S(1)}, u32[]{:S(2)}, u32[]{:S(2)}) %all-to-all-start) | async-done | bytes 917536 | tf_op jit(solution)/shard_map/all_to_all | solution.py:119
  99.0 1.5 %shard_map.77 = (bf16[1,2,64,1792]{3,2,1,0:T(8,128)(2,1)}, bf16[2,64,1792]{2,1,0:T(8,128)(2,1)S(1)}, f32[2,64]{1,0:T(2,128)S(1)}) custom-call(bf16[256,1792]{1,0:T(8,128)(2,1)S(1)} %bitcast.46, bf16[64,2304]{1,0:T(8,128)(2,1)S(1)} %collective-permute-done.4.side0_ref, bf16[64,2304]{1,0:T(8,128)(2,1)S(1)} %collective-permute-done.5.side1_ref), custom_call_target="tpu_custom_call" | custom-call | flops 234881024 | bytes 917504 | tf_op jit(solution)/shard_map/pallas_call | solution.py:65
  100.5 9.7 %all-gather.1.totals_ref = f32[4,2,64]{2,1,0:T(2,128)S(1)} all-gather(f32[1,2,64]{2,1,0:T(2,128)S(1)} %bitcast.47), channel_id=2, replica_groups=mesh['pipe'=8,'expert'=32,'dp'=4] {'dp'}, dimensions={0}, use_global_device_ids=true | all-gather | bytes 2560 | tf_op jit(solution)/shard_map/all_gather | solution.py:130
  110.3 1.0 shard_map.78
  (8 shorter events, 0.1 us)
Async XLA Ops:
  0.6 1.5 %copy-start = (bf16[1,512,1792]{2,1,0:T(8,128)(2,1)S(1)}, bf16[1,512,1792]{2,1,0:T(8,128)(2,1)}, u32[]{:S(2)}) copy-start(bf16[1,512,1792]{2,1,0:T(8,128)(2,1)} %param.10) | copy-start | bytes 5505028
  0.6 4.8 %copy-start.1 = (bf16[1,2,256,512]{3,2,1,0:T(8,128)(2,1)S(1)}, bf16[1,2,256,512]{3,2,1,0:T(8,128)(2,1)}, u32[]{:S(2)}) copy-start(bf16[1,2,256,512]{3,2,1,0:T(8,128)(2,1)} %param.9) | copy-start | bytes 1572868
  3.5 14.7 %collective-permute-start = (bf16[128,1792]{1,0:T(8,128)(2,1)S(1)}, bf16[128,1792]{1,0:T(8,128)(2,1)S(1)}, u32[]{:S(2)}, u32[]{:S(2)}) collective-permute-start(bf16[128,1792]{1,0:T(8,128)(2,1)S(1)} %convolution_convert_fusion.3), channel_id=1, source_target_pairs={{0,132},{4,128},{8,140},{12,136},{16,148},{20,144},{24,156},{28,15... | collective-permute-start | bytes 1376264 | tf_op jit(solution)/shard_map/ppermute | solution.py:27
  6.6 13.8 %collective-permute-start.1 = (bf16[128,1792]{1,0:T(8,128)(2,1)}, bf16[128,1792]{1,0:T(8,128)(2,1)}, u32[]{:S(2)}, u32[]{:S(2)}) collective-permute-start(bf16[128,1792]{1,0:T(8,128)(2,1)} %convolution_convert_fusion.2), channel_id=1, source_target_pairs={{0,128},{128,256},{256,384},{384,512},{512,640},{640,768},{768,896... | collective-permute-start | bytes 1376264 | tf_op jit(solution)/shard_map/ppermute | solution.py:16
  9.7 18.3 %collective-permute-start.2 = (bf16[128,1792]{1,0:T(8,128)(2,1)S(1)}, bf16[128,1792]{1,0:T(8,128)(2,1)S(1)}, u32[]{:S(2)}, u32[]{:S(2)}) collective-permute-start(bf16[128,1792]{1,0:T(8,128)(2,1)S(1)} %convolution_convert_fusion.1), channel_id=1, source_target_pairs={{128,4},{132,0},{136,12},{140,8},{144,20},{148,16},{152,28},{156,2... | collective-permute-start | bytes 1376264 | tf_op jit(solution)/shard_map/ppermute | solution.py:27
  13.9 14.1 %collective-permute-start.3 = (bf16[128,1792]{1,0:T(8,128)(2,1)S(1)}, bf16[128,1792]{1,0:T(8,128)(2,1)S(1)}, u32[]{:S(2)}, u32[]{:S(2)}) collective-permute-start(bf16[128,1792]{1,0:T(8,128)(2,1)S(1)} %convolution_convert_fusion), channel_id=1, source_target_pairs={{128,0},{256,128},{384,256},{512,384},{640,512},{768,640},{896,768... | collective-permute-start | bytes 1376264 | tf_op jit(solution)/shard_map/ppermute | solution.py:16
  28.1 22.0 %copy-start.3 = (s32[1,2,64,8]{2,3,1,0:T(8,128)S(1)}, s32[1,2,64,8]{2,3,1,0:T(8,128)}, u32[]{:S(2)}) copy-start(s32[1,2,64,8]{2,3,1,0:T(8,128)} %param.7) | copy-start | bytes 12292
  28.1 22.2 %copy-start.4 = (f32[1,2,64,8]{2,3,1,0:T(8,128)S(1)}, f32[1,2,64,8]{2,3,1,0:T(8,128)}, u32[]{:S(2)}) copy-start(f32[1,2,64,8]{2,3,1,0:T(8,128)} %param.8) | copy-start | bytes 12292
  28.2 23.4 %copy-start.2 = (bf16[1,2,64,1792]{3,2,1,0:T(8,128)(2,1)S(1)}, bf16[1,2,64,1792]{3,2,1,0:T(8,128)(2,1)}, u32[]{:S(2)}) copy-start(bf16[1,2,64,1792]{3,2,1,0:T(8,128)(2,1)} %param.6) | copy-start | bytes 1376260
  29.2 69.8 %all-to-all-start = ((bf16[16,2,8,1792]{3,2,1,0:T(8,128)(2,1)}), bf16[16,2,8,1792]{3,2,1,0:T(8,128)(2,1)S(1)}, u32[]{:S(2)}, u32[]{:S(2)}) async-start(bf16[16,2,8,1792]{3,2,1,0:T(8,128)(2,1)} %pad_maximum_fusion), calls=%async_computation | async-start | bytes 1835008 | tf_op jit(solution)/shard_map/all_to_all | solution.py:119
  52.3 8.4 %collective-permute-start.5 = (bf16[64,2304]{1,0:T(8,128)(2,1)}, bf16[64,2304]{1,0:T(8,128)(2,1)S(1)}, u32[]{:S(2)}, u32[]{:S(2)}) collective-permute-start(bf16[64,2304]{1,0:T(8,128)(2,1)} %pad_maximum_fusion.2), channel_id=1, source_target_pairs={{128,0},{256,128},{384,256},{512,384},{640,512},{768,640},{896,768... | collective-permute-start | bytes 884744 | tf_op jit(solution)/shard_map/ppermute | solution.py:16
  56.0 9.9 %collective-permute-start.4 = (bf16[64,2304]{1,0:T(8,128)(2,1)}, bf16[64,2304]{1,0:T(8,128)(2,1)S(1)}, u32[]{:S(2)}, u32[]{:S(2)}) collective-permute-start(bf16[64,2304]{1,0:T(8,128)(2,1)} %pad_maximum_fusion.1), channel_id=1, source_target_pairs={{0,128},{128,256},{256,384},{384,512},{512,640},{640,768},{768,896... | collective-permute-start | bytes 884744 | tf_op jit(solution)/shard_map/ppermute | solution.py:16

commit v4 on v3

--- a/solution.py
+++ b/solution.py
@@ -44,20 +44,19 @@
     return lax.broadcasted_iota(jnp.int32, (size, size), 0) == lax.broadcasted_iota(jnp.int32, (size, size), 1)
 
 
-def combine_kernel(received_ref, side0_ref, side1_ref, out_ref, copy_ref, squares_ref):
-    received = received_ref[...]
-    slots, columns = received.shape
-    for m, side_ref in enumerate((side0_ref, side1_ref)):
-        high = side_ref[:, columns : columns + slots]
-        low = side_ref[:, columns + slots :]
-        combined = jnp.dot(high, received, preferred_element_type=jnp.float32)
-        combined += jnp.dot(low, received, preferred_element_type=jnp.float32)
-        layer_out = (side_ref[:, :columns].astype(jnp.float32) + combined).astype(jnp.bfloat16)
-        out_ref[0, m] = layer_out
-        copy_ref[m] = layer_out
+def combine_kernel(received_ref, side0_ref, side1_ref, rows_ref, squares_ref):
+    slots, columns = received_ref.shape
+    tokens = side0_ref.shape[0]
+    sides = (side0_ref, side1_ref)
+    weights = [side[:, start : start + slots] for side in sides for start in (columns, columns + slots)]
+    products = jnp.dot(jnp.concatenate(weights, axis=0), received_ref[...], preferred_element_type=jnp.float32)
+    for m, side in enumerate(sides):
+        high, low = (products[part * tokens : (part + 1) * tokens] for part in (2 * m, 2 * m + 1))
+        layer_out = (side[:, :columns].astype(jnp.float32) + (high + low)).astype(jnp.bfloat16)
+        rows_ref[m] = layer_out
         floats = layer_out.astype(jnp.float32)
         total = jnp.sum(floats * floats, axis=1, keepdims=True)
-        squares_ref[m : m + 1] = jnp.sum(jnp.where(on_diagonal(floats.shape[0]), total, 0.0), axis=0, keepdims=True)
+        squares_ref[m : m + 1] = jnp.sum(jnp.where(on_diagonal(tokens), total, 0.0), axis=0, keepdims=True)
 
 
 def combine(received, sides, tokens):
@@ -65,7 +64,6 @@
     return pl.pallas_call(
         combine_kernel,
         out_shape=(
-            jax.ShapeDtypeStruct((1, 2, tokens, columns), jnp.bfloat16),
             jax.ShapeDtypeStruct((2, tokens, columns), jnp.bfloat16),
             jax.ShapeDtypeStruct((2, tokens), jnp.float32),
         ),
@@ -76,20 +74,22 @@
     )(received, *sides)
 
 
-def norm_kernel(rows_ref, totals_ref, gains_ref, out_ref):
+def norm_kernel(rows_ref, totals_ref, gains_ref, stream_ref, normed_ref):
     tokens, columns = rows_ref.shape[1:]
     totals = jnp.sum(totals_ref[...], axis=0)
     for m in range(2):
         total = jnp.sum(jnp.where(on_diagonal(tokens), totals[m : m + 1], 0.0), axis=1, keepdims=True)
         factor = lax.rsqrt(total / D + EPSILON)
         normed = rows_ref[m].astype(jnp.float32) * factor * gains_ref[m : m + 1]
-        out_ref[0, m] = normed.astype(jnp.bfloat16)
+        stream_ref[0, m] = rows_ref[m]
+        normed_ref[0, m] = normed.astype(jnp.bfloat16)
 
 
 def normalize(rows, totals, gains):
+    shape = jax.ShapeDtypeStruct((1, *rows.shape), jnp.bfloat16)
     return pl.pallas_call(
         norm_kernel,
-        out_shape=jax.ShapeDtypeStruct((1, *rows.shape), jnp.bfloat16),
+        out_shape=(shape, shape),
         cost_estimate=pl.CostEstimate(flops=4 * rows.size, bytes_accessed=4 * rows.size, transcendentals=0),
         compiler_params=pltpu.CompilerParams(vmem_limit_bytes=8 << 20),
     )(rows, totals, gains)
@@ -106,6 +106,8 @@
     hidden = expert_hidden[0].reshape(2, experts, 2, CAPACITY, -1)
     kept = lax.dynamic_index_in_dim(hidden, parity, 2, keepdims=False).reshape(2, experts * CAPACITY, -1)
     sent = lax.dynamic_index_in_dim(hidden, 1 - parity, 2, keepdims=False).reshape(2, experts * CAPACITY, -1)
+
+    kept, sent = lax.optimization_barrier((kept, sent))
 
     def project(rows):
         return jnp.dot(rows, down_weight[0], preferred_element_type=jnp.float32).astype(jnp.bfloat16)
@@ -126,7 +128,7 @@
         low = (weights - high.astype(jnp.float32)).astype(jnp.bfloat16)
         sides.append(shifted(jnp.concatenate([stream[0, m], high, low], axis=1), distance))
     received = exchanged.reshape(experts * 2 * CAPACITY, columns)
-    next_stream, rows, squares = combine(received, sides, tokens)
+    rows, squares = combine(received, sides, tokens)
     totals = lax.all_gather(squares, "dp")
     gains = jnp.stack(
         [
@@ -134,7 +136,7 @@
             for distance in (1, -1)
         ]
     )
-    return (next_stream, normalize(rows, totals, gains))
+    return normalize(rows, totals, gains)
 
 
 def solution(mesh):

time: 112 us -> 109 us (0.973)
  waiting for transfers between devices: 49.8 us -> 51.8 us
  matrix products: 3.75 us -> 2.08 us
    ppermute x2, waiting for transfers between devices: 7.42 us -> 10.5 us  [shifted_to_partner(): return lax.ppermute(block, ('pipe', 'expert'), route)]
    dot_general x4, matrix products: 3.33 us -> 1.67 us  [project(): jnp.dot(rows, down_weight[0], preferred_element_type=jnp.float32)]
    reshape x0 -> x1, local copies, waits for them, and re-layouts: none -> 1.2 us  [per_device(): lax.dynamic_index_in_dim(hidden, 1 - parity, 2, keepdims=False)]
  transfers between devices with their start and end apart: 7 -> 7, of which waited for: 6 -> 6; matrix products, arithmetic and copies ran while one was open for 6% -> 5% of each run, Pallas kernels for 0% -> 0%
where the time goes in v4:
time: 109 us
  waiting for transfers between devices  51.8 us (48%)
  starting transfers between devices  36.3 us (33%)
  blocking collectives  9.72 us (9%)
  other arithmetic  3.51 us (3%)
  local copies, waits for them, and re-layouts  2.94 us (3%)
  matrix products  2.08 us (2%)
  Pallas kernels  1.52 us (1%)
    all_to_all x1, waiting for transfers between devices, per_device(): lax.all_to_all(jnp.stack(sums, axis=1), 'expert', 0, 0, axis_index_groups...  32.5 us
    all_to_all x1, starting transfers between devices, per_device(): lax.all_to_all(jnp.stack(sums, axis=1), 'expert', 0, 0, axis_index_groups...  21 us
    ppermute x2, waiting for transfers between devices, shifted_to_partner(): return lax.ppermute(block, ('pipe', 'expert'), route)  10.5 us
    all_gather x1, blocking collectives, per_device(): totals = lax.all_gather(squares, 'dp')  9.72 us
    ppermute x4, starting transfers between devices, shifted(): return lax.ppermute(block, 'pipe', route)  9.58 us
    ppermute x4, waiting for transfers between devices, shifted(): return lax.ppermute(block, 'pipe', route)  8.83 us
    ppermute x2, starting transfers between devices, shifted_to_partner(): return lax.ppermute(block, ('pipe', 'expert'), route)  5.7 us
  transfers between devices with their start and end apart: 7, of which 6 were waited for; matrix products, arithmetic and copies ran while one was open for 5% of the time, Pallas kernels for 0%

profile of v4, /device:TPU:200, one launch (start us, length us, event | category | flops | bytes accessed | tf_op | source)
XLA Modules:
  0.0 108.7 jit_solution(5294064024898855140)
XLA Ops:
  0.6 0.0 copy-start
  0.7 1.2 %dynamic-slice_bitcast_fusion = (bf16[2,128,512]{2,1,0:T(8,128)(2,1)S(1)}, bf16[2,128,512]{2,1,0:T(8,128)(2,1)S(1)}) fusion(bf16[2,16,2,8,512]{4,3,2,1,0:T(8,128)(2,1)} %bitcast.52, s32[]{:T(128)S(6)} %select_n.79, s32[]{:T(128)S(6)} %select_n.78), kind=kLoop, calls=%fused_computation.29 | loop fusion | bytes 1048584 | tf_op jit(solution)/shard_map/reshape | solution.py:108
  1.9 0.4 copy-done
  2.3 0.4 convolution_convert_fusion.3
  2.7 1.9 %collective-permute-start = (bf16[128,1792]{1,0:T(8,128)(2,1)S(1)}, bf16[128,1792]{1,0:T(8,128)(2,1)S(1)}, u32[]{:S(2)}, u32[]{:S(2)}) collective-permute-start(bf16[128,1792]{1,0:T(8,128)(2,1)S(1)} %convolution_convert_fusion.3), channel_id=1, source_target_pairs={{0,132},{4,128},{8,140},{12,136},{16,148},{20,144},{24,156},{28,15... | collective-permute-start | bytes 1376264 | tf_op jit(solution)/shard_map/ppermute | solution.py:27
  4.6 0.4 convolution_convert_fusion.2
  5.1 2.7 %collective-permute-start.1 = (bf16[128,1792]{1,0:T(8,128)(2,1)S(1)}, bf16[128,1792]{1,0:T(8,128)(2,1)S(1)}, u32[]{:S(2)}, u32[]{:S(2)}) collective-permute-start(bf16[128,1792]{1,0:T(8,128)(2,1)S(1)} %convolution_convert_fusion.2), channel_id=1, source_target_pairs={{0,128},{128,256},{256,384},{384,512},{512,640},{640,768},{768,896... | collective-permute-start | bytes 1376264 | tf_op jit(solution)/shard_map/ppermute | solution.py:16
  7.8 0.4 convolution_convert_fusion.1
  8.2 3.8 %collective-permute-start.2 = (bf16[128,1792]{1,0:T(8,128)(2,1)S(1)}, bf16[128,1792]{1,0:T(8,128)(2,1)S(1)}, u32[]{:S(2)}, u32[]{:S(2)}) collective-permute-start(bf16[128,1792]{1,0:T(8,128)(2,1)S(1)} %convolution_convert_fusion.1), channel_id=1, source_target_pairs={{128,4},{132,0},{136,12},{140,8},{144,20},{148,16},{152,28},{156,2... | collective-permute-start | bytes 1376264 | tf_op jit(solution)/shard_map/ppermute | solution.py:27
  12.0 0.4 convolution_convert_fusion
  12.4 2.6 %collective-permute-start.3 = (bf16[128,1792]{1,0:T(8,128)(2,1)S(1)}, bf16[128,1792]{1,0:T(8,128)(2,1)S(1)}, u32[]{:S(2)}, u32[]{:S(2)}) collective-permute-start(bf16[128,1792]{1,0:T(8,128)(2,1)S(1)} %convolution_convert_fusion), channel_id=1, source_target_pairs={{128,0},{256,128},{384,256},{512,384},{640,512},{768,640},{896,768... | collective-permute-start | bytes 1376264 | tf_op jit(solution)/shard_map/ppermute | solution.py:16
  15.0 2.4 %collective-permute-done = bf16[128,1792]{1,0:T(8,128)(2,1)S(1)} collective-permute-done((bf16[128,1792]{1,0:T(8,128)(2,1)S(1)}, bf16[128,1792]{1,0:T(8,128)(2,1)S(1)}, u32[]{:S(2)}, u32[]{:S(2)}) %collective-permute-start) | collective-permute-done | bytes 458784 | tf_op jit(solution)/shard_map/ppermute | solution.py:27
  17.4 1.6 %collective-permute-done.1 = bf16[128,1792]{1,0:T(8,128)(2,1)S(1)} collective-permute-done((bf16[128,1792]{1,0:T(8,128)(2,1)S(1)}, bf16[128,1792]{1,0:T(8,128)(2,1)S(1)}, u32[]{:S(2)}, u32[]{:S(2)}) %collective-permute-start.1) | collective-permute-done | bytes 458784 | tf_op jit(solution)/shard_map/ppermute | solution.py:16
  19.1 0.1 fusion.12
  19.2 8.1 %collective-permute-done.2 = bf16[128,1792]{1,0:T(8,128)(2,1)S(1)} collective-permute-done((bf16[128,1792]{1,0:T(8,128)(2,1)S(1)}, bf16[128,1792]{1,0:T(8,128)(2,1)S(1)}, u32[]{:S(2)}, u32[]{:S(2)}) %collective-permute-start.2) | collective-permute-done | bytes 458784 | tf_op jit(solution)/shard_map/ppermute | solution.py:27
  27.3 0.0 collective-permute-done.3
  27.3 0.1 fusion.13
  27.4 0.0 copy-start.2
  27.4 0.0 copy-start.3
  27.4 0.0 copy-start.1
  27.4 1.0 pad_maximum_fusion
  28.4 21.0 %all-to-all-start = ((bf16[16,2,8,1792]{3,2,1,0:T(8,128)(2,1)}), bf16[16,2,8,1792]{3,2,1,0:T(8,128)(2,1)S(1)}, u32[]{:S(2)}, u32[]{:S(2)}) async-start(bf16[16,2,8,1792]{3,2,1,0:T(8,128)(2,1)} %pad_maximum_fusion), calls=%async_computation | async-start | bytes 1835008 | tf_op jit(solution)/shard_map/all_to_all | solution.py:121
  49.4 0.0 copy-done.2
  49.4 0.1 copy.22
  49.5 0.1 copy.24
  49.6 0.0 copy-done.3
  49.6 0.1 copy.23
  49.7 0.1 copy.25
  49.8 0.4 compare_reduce_fusion
  50.2 0.4 fusion.11
  50.6 0.2 subtract_convert_fusion
  50.8 0.0 copy-done.1
  50.8 0.7 pad_maximum_fusion.2
  51.6 2.1 %collective-permute-start.5 = (bf16[64,2304]{1,0:T(8,128)(2,1)}, bf16[64,2304]{1,0:T(8,128)(2,1)S(1)}, u32[]{:S(2)}, u32[]{:S(2)}) collective-permute-start(bf16[64,2304]{1,0:T(8,128)(2,1)} %pad_maximum_fusion.2), channel_id=1, source_target_pairs={{128,0},{256,128},{384,256},{512,384},{640,512},{768,640},{896,768... | collective-permute-start | bytes 884744 | tf_op jit(solution)/shard_map/ppermute | solution.py:16
  53.7 0.2 subtract_convert_fusion.1
  53.9 0.7 pad_maximum_fusion.1
  54.7 2.2 %collective-permute-start.4 = (bf16[64,2304]{1,0:T(8,128)(2,1)}, bf16[64,2304]{1,0:T(8,128)(2,1)S(1)}, u32[]{:S(2)}, u32[]{:S(2)}) collective-permute-start(bf16[64,2304]{1,0:T(8,128)(2,1)} %pad_maximum_fusion.1), channel_id=1, source_target_pairs={{0,128},{128,256},{256,384},{384,512},{512,640},{640,768},{768,896... | collective-permute-start | bytes 884744 | tf_op jit(solution)/shard_map/ppermute | solution.py:16
  56.9 0.9 constant_dynamic-slice_fusion.1
  57.8 4.9 %collective-permute-done.5.side1_ref = bf16[64,2304]{1,0:T(8,128)(2,1)S(1)} collective-permute-done((bf16[64,2304]{1,0:T(8,128)(2,1)}, bf16[64,2304]{1,0:T(8,128)(2,1)S(1)}, u32[]{:S(2)}, u32[]{:S(2)}) %collective-permute-start.5) | collective-permute-done | bytes 294944 | tf_op jit(solution)/shard_map/ppermute | solution.py:16
  62.7 2.3 %collective-permute-done.4.side0_ref = bf16[64,2304]{1,0:T(8,128)(2,1)S(1)} collective-permute-done((bf16[64,2304]{1,0:T(8,128)(2,1)}, bf16[64,2304]{1,0:T(8,128)(2,1)S(1)}, u32[]{:S(2)}, u32[]{:S(2)}) %collective-permute-start.4) | collective-permute-done | bytes 294944 | tf_op jit(solution)/shard_map/ppermute | solution.py:16
  65.0 32.5 %all-to-all-done = bf16[16,2,8,1792]{3,2,1,0:T(8,128)(2,1)S(1)} async-done(((bf16[16,2,8,1792]{3,2,1,0:T(8,128)(2,1)}), bf16[16,2,8,1792]{3,2,1,0:T(8,128)(2,1)S(1)}, u32[]{:S(2)}, u32[]{:S(2)}) %all-to-all-start) | async-done | bytes 917536 | tf_op jit(solution)/shard_map/all_to_all | solution.py:121
  97.5 0.5 shard_map.77
  98.0 9.7 %all-gather.1.totals_ref = f32[4,2,64]{2,1,0:T(2,128)S(1)} all-gather(f32[1,2,64]{2,1,0:T(2,128)S(1)} %bitcast.51), channel_id=2, replica_groups=mesh['pipe'=8,'expert'=32,'dp'=4] {'dp'}, dimensions={0}, use_global_device_ids=true | all-gather | bytes 2560 | tf_op jit(solution)/shard_map/all_gather | solution.py:132
  107.7 1.0 shard_map.78
  (8 shorter events, 0.1 us)
Async XLA Ops:
  0.6 1.7 %copy-start = (bf16[1,512,1792]{2,1,0:T(8,128)(2,1)S(1)}, bf16[1,512,1792]{2,1,0:T(8,128)(2,1)}, u32[]{:S(2)}) copy-start(bf16[1,512,1792]{2,1,0:T(8,128)(2,1)} %param.10) | copy-start | bytes 5505028
  2.7 14.7 %collective-permute-start = (bf16[128,1792]{1,0:T(8,128)(2,1)S(1)}, bf16[128,1792]{1,0:T(8,128)(2,1)S(1)}, u32[]{:S(2)}, u32[]{:S(2)}) collective-permute-start(bf16[128,1792]{1,0:T(8,128)(2,1)S(1)} %convolution_convert_fusion.3), channel_id=1, source_target_pairs={{0,132},{4,128},{8,140},{12,136},{16,148},{20,144},{24,156},{28,15... | collective-permute-start | bytes 1376264 | tf_op jit(solution)/shard_map/ppermute | solution.py:27
  5.1 14.0 %collective-permute-start.1 = (bf16[128,1792]{1,0:T(8,128)(2,1)S(1)}, bf16[128,1792]{1,0:T(8,128)(2,1)S(1)}, u32[]{:S(2)}, u32[]{:S(2)}) collective-permute-start(bf16[128,1792]{1,0:T(8,128)(2,1)S(1)} %convolution_convert_fusion.2), channel_id=1, source_target_pairs={{0,128},{128,256},{256,384},{384,512},{512,640},{640,768},{768,896... | collective-permute-start | bytes 1376264 | tf_op jit(solution)/shard_map/ppermute | solution.py:16
  8.2 19.1 %collective-permute-start.2 = (bf16[128,1792]{1,0:T(8,128)(2,1)S(1)}, bf16[128,1792]{1,0:T(8,128)(2,1)S(1)}, u32[]{:S(2)}, u32[]{:S(2)}) collective-permute-start(bf16[128,1792]{1,0:T(8,128)(2,1)S(1)} %convolution_convert_fusion.1), channel_id=1, source_target_pairs={{128,4},{132,0},{136,12},{140,8},{144,20},{148,16},{152,28},{156,2... | collective-permute-start | bytes 1376264 | tf_op jit(solution)/shard_map/ppermute | solution.py:27
  12.4 14.9 %collective-permute-start.3 = (bf16[128,1792]{1,0:T(8,128)(2,1)S(1)}, bf16[128,1792]{1,0:T(8,128)(2,1)S(1)}, u32[]{:S(2)}, u32[]{:S(2)}) collective-permute-start(bf16[128,1792]{1,0:T(8,128)(2,1)S(1)} %convolution_convert_fusion), channel_id=1, source_target_pairs={{128,0},{256,128},{384,256},{512,384},{640,512},{768,640},{896,768... | collective-permute-start | bytes 1376264 | tf_op jit(solution)/shard_map/ppermute | solution.py:16
  27.4 22.0 %copy-start.2 = (s32[1,2,64,8]{2,3,1,0:T(8,128)S(1)}, s32[1,2,64,8]{2,3,1,0:T(8,128)}, u32[]{:S(2)}) copy-start(s32[1,2,64,8]{2,3,1,0:T(8,128)} %param.7) | copy-start | bytes 12292
  27.4 22.2 %copy-start.3 = (f32[1,2,64,8]{2,3,1,0:T(8,128)S(1)}, f32[1,2,64,8]{2,3,1,0:T(8,128)}, u32[]{:S(2)}) copy-start(f32[1,2,64,8]{2,3,1,0:T(8,128)} %param.8) | copy-start | bytes 12292
  27.4 23.4 %copy-start.1 = (bf16[1,2,64,1792]{3,2,1,0:T(8,128)(2,1)S(1)}, bf16[1,2,64,1792]{3,2,1,0:T(8,128)(2,1)}, u32[]{:S(2)}) copy-start(bf16[1,2,64,1792]{3,2,1,0:T(8,128)(2,1)} %param.6) | copy-start | bytes 1376260
  28.4 69.1 %all-to-all-start = ((bf16[16,2,8,1792]{3,2,1,0:T(8,128)(2,1)}), bf16[16,2,8,1792]{3,2,1,0:T(8,128)(2,1)S(1)}, u32[]{:S(2)}, u32[]{:S(2)}) async-start(bf16[16,2,8,1792]{3,2,1,0:T(8,128)(2,1)} %pad_maximum_fusion), calls=%async_computation | async-start | bytes 1835008 | tf_op jit(solution)/shard_map/all_to_all | solution.py:121
  51.6 11.1 %collective-permute-start.5 = (bf16[64,2304]{1,0:T(8,128)(2,1)}, bf16[64,2304]{1,0:T(8,128)(2,1)S(1)}, u32[]{:S(2)}, u32[]{:S(2)}) collective-permute-start(bf16[64,2304]{1,0:T(8,128)(2,1)} %pad_maximum_fusion.2), channel_id=1, source_target_pairs={{128,0},{256,128},{384,256},{512,384},{640,512},{768,640},{896,768... | collective-permute-start | bytes 884744 | tf_op jit(solution)/shard_map/ppermute | solution.py:16
  54.7 10.3 %collective-permute-start.4 = (bf16[64,2304]{1,0:T(8,128)(2,1)}, bf16[64,2304]{1,0:T(8,128)(2,1)S(1)}, u32[]{:S(2)}, u32[]{:S(2)}) collective-permute-start(bf16[64,2304]{1,0:T(8,128)(2,1)} %pad_maximum_fusion.1), channel_id=1, source_target_pairs={{0,128},{128,256},{256,384},{384,512},{512,640},{640,768},{768,896... | collective-permute-start | bytes 884744 | tf_op jit(solution)/shard_map/ppermute | solution.py:16

commit v5 on v4

--- a/solution.py
+++ b/solution.py
@@ -75,20 +75,30 @@
 
 
 def norm_kernel(rows_ref, totals_ref, gains_ref, stream_ref, normed_ref):
-    tokens, columns = rows_ref.shape[1:]
+    m = pl.program_id(0)
+    tokens = rows_ref.shape[1]
     totals = jnp.sum(totals_ref[...], axis=0)
-    for m in range(2):
-        total = jnp.sum(jnp.where(on_diagonal(tokens), totals[m : m + 1], 0.0), axis=1, keepdims=True)
-        factor = lax.rsqrt(total / D + EPSILON)
-        normed = rows_ref[m].astype(jnp.float32) * factor * gains_ref[m : m + 1]
-        stream_ref[0, m] = rows_ref[m]
-        normed_ref[0, m] = normed.astype(jnp.bfloat16)
+    own = jnp.where(m == 0, totals[:1], totals[1:])
+    gain = jnp.where(m == 0, gains_ref[:1], gains_ref[1:])
+    total = jnp.sum(jnp.where(on_diagonal(tokens), own, 0.0), axis=1, keepdims=True)
+    factor = lax.rsqrt(total / D + EPSILON)
+    rows = rows_ref[0]
+    stream_ref[0, 0] = rows
+    normed_ref[0, 0] = (rows.astype(jnp.float32) * factor * gain).astype(jnp.bfloat16)
 
 
 def normalize(rows, totals, gains):
     shape = jax.ShapeDtypeStruct((1, *rows.shape), jnp.bfloat16)
+    out = pl.BlockSpec((1, 1, *rows.shape[1:]), lambda m: (0, m, 0, 0))
     return pl.pallas_call(
         norm_kernel,
+        grid=(2,),
+        in_specs=[
+            pl.BlockSpec((1, *rows.shape[1:]), lambda m: (m, 0, 0)),
+            pl.BlockSpec(totals.shape, lambda m: (0, 0, 0)),
+            pl.BlockSpec(gains.shape, lambda m: (0, 0)),
+        ],
+        out_specs=(out, out),
         out_shape=(shape, shape),
         cost_estimate=pl.CostEstimate(flops=4 * rows.size, bytes_accessed=4 * rows.size, transcendentals=0),
         compiler_params=pltpu.CompilerParams(vmem_limit_bytes=8 << 20),
@@ -112,15 +122,17 @@
     def project(rows):
         return jnp.dot(rows, down_weight[0], preferred_element_type=jnp.float32).astype(jnp.bfloat16)
 
-    sums = []
+    rows = None
     for m, distance in enumerate((1, -1)):
         theirs = shifted_to_partner(project(sent[m]), distance)
         own = shifted(project(kept[m]), distance)
         total = (theirs.astype(jnp.float32) + own.astype(jnp.float32)).astype(jnp.bfloat16)
-        sums.append(total.reshape(experts, CAPACITY, columns))
-    exchanged = lax.all_to_all(
-        jnp.stack(sums, axis=1), "expert", 0, 0, axis_index_groups=halves, tiled=True
-    )
+        total = total.reshape(experts, 1, CAPACITY, columns)
+        if rows is None:
+            rows = lax.optimization_barrier(jnp.concatenate([total, total], axis=1))
+        else:
+            rows = lax.dynamic_update_slice(rows, total, (0, m, 0, 0))
+    exchanged = lax.all_to_all(rows, "expert", 0, 0, axis_index_groups=halves, tiled=True)
     sides = []
     for m, distance in enumerate((1, -1)):
         weights = route_weights(routes[0, m], gates[0, m], experts, m)

time: 109 us -> 109 us (level)
    another operation x3 -> x0, other arithmetic: 1.22 us -> none  [per_device(): jnp.stack(sums, axis=1)]
  transfers between devices with their start and end apart: 7 -> 7, of which waited for: 6 -> 6; matrix products, arithmetic and copies ran while one was open for 5% -> 6% of each run, Pallas kernels for 0% -> 0%
where the time goes in v5:
time: 109 us; the launch traced here: 108 us
  waiting for transfers between devices  50.9 us (47%)
  starting transfers between devices  36.3 us (33%)
  blocking collectives  9.72 us (9%)
  other arithmetic  4.27 us (4%)
  local copies, waits for them, and re-layouts  2.93 us (3%)
  matrix products  2.08 us (2%)
  Pallas kernels  1.5 us (1%)
    all_to_all x1, waiting for transfers between devices, per_device(): lax.all_to_all(rows, 'expert', 0, 0, axis_index_groups=halves, tiled=True)  32.5 us
    all_to_all x1, starting transfers between devices, per_device(): lax.all_to_all(rows, 'expert', 0, 0, axis_index_groups=halves, tiled=True)  21 us
    all_gather x1, blocking collectives, per_device(): totals = lax.all_gather(squares, 'dp')  9.72 us
    ppermute x4, starting transfers between devices, shifted(): return lax.ppermute(block, 'pipe', route)  9.58 us
    ppermute x2, waiting for transfers between devices, shifted_to_partner(): return lax.ppermute(block, ('pipe', 'expert'), route)  9.55 us
    ppermute x4, waiting for transfers between devices, shifted(): return lax.ppermute(block, 'pipe', route)  8.83 us
    ppermute x2, starting transfers between devices, shifted_to_partner(): return lax.ppermute(block, ('pipe', 'expert'), route)  5.7 us
  transfers between devices with their start and end apart: 7, of which 6 were waited for; matrix products, arithmetic and copies ran while one was open for 6% of the time, Pallas kernels for 0%

profile of v5, /device:TPU:200, one launch (start us, length us, event | category | flops | bytes accessed | tf_op | source)
XLA Modules:
  0.0 108.5 jit_solution(18330641545479683954)
XLA Ops:
  0.6 0.0 copy-start
  0.7 1.2 %dynamic-slice_bitcast_fusion = (bf16[2,128,512]{2,1,0:T(8,128)(2,1)S(1)}, bf16[2,128,512]{2,1,0:T(8,128)(2,1)S(1)}) fusion(bf16[2,16,2,8,512]{4,3,2,1,0:T(8,128)(2,1)} %bitcast.55, s32[]{:T(128)S(6)} %select_n.79, s32[]{:T(128)S(6)} %select_n.78), kind=kLoop, calls=%fused_computation.30 | loop fusion | bytes 1048584 | tf_op jit(solution)/shard_map/reshape | solution.py:118
  1.9 0.4 copy-done
  2.3 0.4 convolution_convert_fusion.3
  2.7 1.9 %collective-permute-start = (bf16[128,1792]{1,0:T(8,128)(2,1)S(1)}, bf16[128,1792]{1,0:T(8,128)(2,1)S(1)}, u32[]{:S(2)}, u32[]{:S(2)}) collective-permute-start(bf16[128,1792]{1,0:T(8,128)(2,1)S(1)} %convolution_convert_fusion.3), channel_id=1, source_target_pairs={{0,132},{4,128},{8,140},{12,136},{16,148},{20,144},{24,156},{28,15... | collective-permute-start | bytes 1376264 | tf_op jit(solution)/shard_map/ppermute | solution.py:27
  4.6 0.4 convolution_convert_fusion.2
  5.1 2.7 %collective-permute-start.1 = (bf16[128,1792]{1,0:T(8,128)(2,1)S(1)}, bf16[128,1792]{1,0:T(8,128)(2,1)S(1)}, u32[]{:S(2)}, u32[]{:S(2)}) collective-permute-start(bf16[128,1792]{1,0:T(8,128)(2,1)S(1)} %convolution_convert_fusion.2), channel_id=1, source_target_pairs={{0,128},{128,256},{256,384},{384,512},{512,640},{640,768},{768,896... | collective-permute-start | bytes 1376264 | tf_op jit(solution)/shard_map/ppermute | solution.py:16
  7.8 0.4 convolution_convert_fusion.1
  8.2 3.8 %collective-permute-start.2 = (bf16[128,1792]{1,0:T(8,128)(2,1)S(1)}, bf16[128,1792]{1,0:T(8,128)(2,1)S(1)}, u32[]{:S(2)}, u32[]{:S(2)}) collective-permute-start(bf16[128,1792]{1,0:T(8,128)(2,1)S(1)} %convolution_convert_fusion.1), channel_id=1, source_target_pairs={{128,4},{132,0},{136,12},{140,8},{144,20},{148,16},{152,28},{156,2... | collective-permute-start | bytes 1376264 | tf_op jit(solution)/shard_map/ppermute | solution.py:27
  12.0 0.4 convolution_convert_fusion
  12.4 2.6 %collective-permute-start.3 = (bf16[128,1792]{1,0:T(8,128)(2,1)S(1)}, bf16[128,1792]{1,0:T(8,128)(2,1)S(1)}, u32[]{:S(2)}, u32[]{:S(2)}) collective-permute-start(bf16[128,1792]{1,0:T(8,128)(2,1)S(1)} %convolution_convert_fusion), channel_id=1, source_target_pairs={{128,0},{256,128},{384,256},{512,384},{640,512},{768,640},{896,768... | collective-permute-start | bytes 1376264 | tf_op jit(solution)/shard_map/ppermute | solution.py:16
  15.0 2.4 %collective-permute-done = bf16[128,1792]{1,0:T(8,128)(2,1)S(1)} collective-permute-done((bf16[128,1792]{1,0:T(8,128)(2,1)S(1)}, bf16[128,1792]{1,0:T(8,128)(2,1)S(1)}, u32[]{:S(2)}, u32[]{:S(2)}) %collective-permute-start) | collective-permute-done | bytes 458784 | tf_op jit(solution)/shard_map/ppermute | solution.py:27
  17.4 1.6 %collective-permute-done.1 = bf16[128,1792]{1,0:T(8,128)(2,1)S(1)} collective-permute-done((bf16[128,1792]{1,0:T(8,128)(2,1)S(1)}, bf16[128,1792]{1,0:T(8,128)(2,1)S(1)}, u32[]{:S(2)}, u32[]{:S(2)}) %collective-permute-start.1) | collective-permute-done | bytes 458784 | tf_op jit(solution)/shard_map/ppermute | solution.py:16
  19.1 0.1 fusion.12
  19.2 1.0 pad_maximum_fusion
  20.1 0.0 copy-start.2
  20.1 0.0 copy-start.3
  20.2 0.0 copy-start.1
  20.2 7.1 %collective-permute-done.2 = bf16[128,1792]{1,0:T(8,128)(2,1)S(1)} collective-permute-done((bf16[128,1792]{1,0:T(8,128)(2,1)S(1)}, bf16[128,1792]{1,0:T(8,128)(2,1)S(1)}, u32[]{:S(2)}, u32[]{:S(2)}) %collective-permute-start.2) | collective-permute-done | bytes 458784 | tf_op jit(solution)/shard_map/ppermute | solution.py:27
  27.3 0.0 collective-permute-done.3
  27.3 0.9 fusion.14
  28.2 21.0 %all-to-all-start = ((bf16[16,2,8,1792]{3,2,1,0:T(8,128)(2,1)}), bf16[16,2,8,1792]{3,2,1,0:T(8,128)(2,1)S(1)}, u32[]{:S(2)}, u32[]{:S(2)}) async-start(bf16[16,2,8,1792]{3,2,1,0:T(8,128)(2,1)} %fusion.14), calls=%async_computation | async-start | bytes 1835008 | tf_op jit(solution)/shard_map/all_to_all | solution.py:135
  49.1 0.0 copy-done.2
  49.2 0.1 copy.25
  49.2 0.1 copy.27
  49.3 0.0 copy-done.3
  49.3 0.1 copy.26
  49.4 0.1 copy.28
  49.5 0.4 compare_reduce_fusion
  49.9 0.4 fusion.11
  50.3 0.2 subtract_convert_fusion
  50.5 0.0 copy-done.1
  50.6 0.7 pad_maximum_fusion.2
  51.3 2.1 %collective-permute-start.5 = (bf16[64,2304]{1,0:T(8,128)(2,1)}, bf16[64,2304]{1,0:T(8,128)(2,1)S(1)}, u32[]{:S(2)}, u32[]{:S(2)}) collective-permute-start(bf16[64,2304]{1,0:T(8,128)(2,1)} %pad_maximum_fusion.2), channel_id=1, source_target_pairs={{128,0},{256,128},{384,256},{512,384},{640,512},{768,640},{896,768... | collective-permute-start | bytes 884744 | tf_op jit(solution)/shard_map/ppermute | solution.py:16
  53.5 0.2 subtract_convert_fusion.1
  53.7 0.7 pad_maximum_fusion.1
  54.4 2.2 %collective-permute-start.4 = (bf16[64,2304]{1,0:T(8,128)(2,1)}, bf16[64,2304]{1,0:T(8,128)(2,1)S(1)}, u32[]{:S(2)}, u32[]{:S(2)}) collective-permute-start(bf16[64,2304]{1,0:T(8,128)(2,1)} %pad_maximum_fusion.1), channel_id=1, source_target_pairs={{0,128},{128,256},{256,384},{384,512},{512,640},{640,768},{768,896... | collective-permute-start | bytes 884744 | tf_op jit(solution)/shard_map/ppermute | solution.py:16
  56.6 0.9 constant_dynamic-slice_fusion.1
  57.6 4.9 %collective-permute-done.5.side1_ref = bf16[64,2304]{1,0:T(8,128)(2,1)S(1)} collective-permute-done((bf16[64,2304]{1,0:T(8,128)(2,1)}, bf16[64,2304]{1,0:T(8,128)(2,1)S(1)}, u32[]{:S(2)}, u32[]{:S(2)}) %collective-permute-start.5) | collective-permute-done | bytes 294944 | tf_op jit(solution)/shard_map/ppermute | solution.py:16
  62.5 2.3 %collective-permute-done.4.side0_ref = bf16[64,2304]{1,0:T(8,128)(2,1)S(1)} collective-permute-done((bf16[64,2304]{1,0:T(8,128)(2,1)}, bf16[64,2304]{1,0:T(8,128)(2,1)S(1)}, u32[]{:S(2)}, u32[]{:S(2)}) %collective-permute-start.4) | collective-permute-done | bytes 294944 | tf_op jit(solution)/shard_map/ppermute | solution.py:16
  64.8 32.5 %all-to-all-done = bf16[16,2,8,1792]{3,2,1,0:T(8,128)(2,1)S(1)} async-done(((bf16[16,2,8,1792]{3,2,1,0:T(8,128)(2,1)}), bf16[16,2,8,1792]{3,2,1,0:T(8,128)(2,1)S(1)}, u32[]{:S(2)}, u32[]{:S(2)}) %all-to-all-start) | async-done | bytes 917536 | tf_op jit(solution)/shard_map/all_to_all | solution.py:135
  97.2 0.5 shard_map.77
  97.7 9.7 %all-gather.1.totals_ref = f32[4,2,64]{2,1,0:T(2,128)S(1)} all-gather(f32[1,2,64]{2,1,0:T(2,128)S(1)} %bitcast.54), channel_id=2, replica_groups=mesh['pipe'=8,'expert'=32,'dp'=4] {'dp'}, dimensions={0}, use_global_device_ids=true | all-gather | bytes 2560 | tf_op jit(solution)/shard_map/all_gather | solution.py:144
  107.5 1.0 shard_map.78
  (8 shorter events, 0.1 us)
Async XLA Ops:
  0.6 1.7 %copy-start = (bf16[1,512,1792]{2,1,0:T(8,128)(2,1)S(1)}, bf16[1,512,1792]{2,1,0:T(8,128)(2,1)}, u32[]{:S(2)}) copy-start(bf16[1,512,1792]{2,1,0:T(8,128)(2,1)} %param.10) | copy-start | bytes 5505028
  2.7 14.7 %collective-permute-start = (bf16[128,1792]{1,0:T(8,128)(2,1)S(1)}, bf16[128,1792]{1,0:T(8,128)(2,1)S(1)}, u32[]{:S(2)}, u32[]{:S(2)}) collective-permute-start(bf16[128,1792]{1,0:T(8,128)(2,1)S(1)} %convolution_convert_fusion.3), channel_id=1, source_target_pairs={{0,132},{4,128},{8,140},{12,136},{16,148},{20,144},{24,156},{28,15... | collective-permute-start | bytes 1376264 | tf_op jit(solution)/shard_map/ppermute | solution.py:27
  5.1 14.0 %collective-permute-start.1 = (bf16[128,1792]{1,0:T(8,128)(2,1)S(1)}, bf16[128,1792]{1,0:T(8,128)(2,1)S(1)}, u32[]{:S(2)}, u32[]{:S(2)}) collective-permute-start(bf16[128,1792]{1,0:T(8,128)(2,1)S(1)} %convolution_convert_fusion.2), channel_id=1, source_target_pairs={{0,128},{128,256},{256,384},{384,512},{512,640},{640,768},{768,896... | collective-permute-start | bytes 1376264 | tf_op jit(solution)/shard_map/ppermute | solution.py:16
  8.2 19.1 %collective-permute-start.2 = (bf16[128,1792]{1,0:T(8,128)(2,1)S(1)}, bf16[128,1792]{1,0:T(8,128)(2,1)S(1)}, u32[]{:S(2)}, u32[]{:S(2)}) collective-permute-start(bf16[128,1792]{1,0:T(8,128)(2,1)S(1)} %convolution_convert_fusion.1), channel_id=1, source_target_pairs={{128,4},{132,0},{136,12},{140,8},{144,20},{148,16},{152,28},{156,2... | collective-permute-start | bytes 1376264 | tf_op jit(solution)/shard_map/ppermute | solution.py:27
  12.4 14.9 %collective-permute-start.3 = (bf16[128,1792]{1,0:T(8,128)(2,1)S(1)}, bf16[128,1792]{1,0:T(8,128)(2,1)S(1)}, u32[]{:S(2)}, u32[]{:S(2)}) collective-permute-start(bf16[128,1792]{1,0:T(8,128)(2,1)S(1)} %convolution_convert_fusion), channel_id=1, source_target_pairs={{128,0},{256,128},{384,256},{512,384},{640,512},{768,640},{896,768... | collective-permute-start | bytes 1376264 | tf_op jit(solution)/shard_map/ppermute | solution.py:16
  20.1 29.0 %copy-start.2 = (s32[1,2,64,8]{2,3,1,0:T(8,128)S(1)}, s32[1,2,64,8]{2,3,1,0:T(8,128)}, u32[]{:S(2)}) copy-start(s32[1,2,64,8]{2,3,1,0:T(8,128)} %param.7) | copy-start | bytes 12292
  20.1 29.2 %copy-start.3 = (f32[1,2,64,8]{2,3,1,0:T(8,128)S(1)}, f32[1,2,64,8]{2,3,1,0:T(8,128)}, u32[]{:S(2)}) copy-start(f32[1,2,64,8]{2,3,1,0:T(8,128)} %param.8) | copy-start | bytes 12292
  20.2 30.4 %copy-start.1 = (bf16[1,2,64,1792]{3,2,1,0:T(8,128)(2,1)S(1)}, bf16[1,2,64,1792]{3,2,1,0:T(8,128)(2,1)}, u32[]{:S(2)}) copy-start(bf16[1,2,64,1792]{3,2,1,0:T(8,128)(2,1)} %param.6) | copy-start | bytes 1376260
  28.2 69.1 %all-to-all-start = ((bf16[16,2,8,1792]{3,2,1,0:T(8,128)(2,1)}), bf16[16,2,8,1792]{3,2,1,0:T(8,128)(2,1)S(1)}, u32[]{:S(2)}, u32[]{:S(2)}) async-start(bf16[16,2,8,1792]{3,2,1,0:T(8,128)(2,1)} %fusion.14), calls=%async_computation | async-start | bytes 1835008 | tf_op jit(solution)/shard_map/all_to_all | solution.py:135
  51.3 11.1 %collective-permute-start.5 = (bf16[64,2304]{1,0:T(8,128)(2,1)}, bf16[64,2304]{1,0:T(8,128)(2,1)S(1)}, u32[]{:S(2)}, u32[]{:S(2)}) collective-permute-start(bf16[64,2304]{1,0:T(8,128)(2,1)} %pad_maximum_fusion.2), channel_id=1, source_target_pairs={{128,0},{256,128},{384,256},{512,384},{640,512},{768,640},{896,768... | collective-permute-start | bytes 884744 | tf_op jit(solution)/shard_map/ppermute | solution.py:16
  54.4 10.3 %collective-permute-start.4 = (bf16[64,2304]{1,0:T(8,128)(2,1)}, bf16[64,2304]{1,0:T(8,128)(2,1)S(1)}, u32[]{:S(2)}, u32[]{:S(2)}) collective-permute-start(bf16[64,2304]{1,0:T(8,128)(2,1)} %pad_maximum_fusion.1), channel_id=1, source_target_pairs={{0,128},{128,256},{256,384},{384,512},{512,640},{640,768},{768,896... | collective-permute-start | bytes 884744 | tf_op jit(solution)/shard_map/ppermute | solution.py:16

commit v6 on v4

--- a/solution.py
+++ b/solution.py
@@ -112,15 +112,17 @@
     def project(rows):
         return jnp.dot(rows, down_weight[0], preferred_element_type=jnp.float32).astype(jnp.bfloat16)
 
-    sums = []
+    rows = None
     for m, distance in enumerate((1, -1)):
         theirs = shifted_to_partner(project(sent[m]), distance)
         own = shifted(project(kept[m]), distance)
         total = (theirs.astype(jnp.float32) + own.astype(jnp.float32)).astype(jnp.bfloat16)
-        sums.append(total.reshape(experts, CAPACITY, columns))
-    exchanged = lax.all_to_all(
-        jnp.stack(sums, axis=1), "expert", 0, 0, axis_index_groups=halves, tiled=True
-    )
+        total = total.reshape(experts, 1, CAPACITY, columns)
+        if rows is None:
+            rows = lax.optimization_barrier(jnp.concatenate([total, total], axis=1))
+        else:
+            rows = lax.dynamic_update_slice(rows, total, (0, m, 0, 0))
+    exchanged = lax.all_to_all(rows, "expert", 0, 0, axis_index_groups=halves, tiled=True)
     sides = []
     for m, distance in enumerate((1, -1)):
         weights = route_weights(routes[0, m], gates[0, m], experts, m)

time: 109 us -> 109 us (level)
    another operation x3 -> x0, other arithmetic: 1.22 us -> none  [per_device(): jnp.stack(sums, axis=1)]
  transfers between devices with their start and end apart: 7 -> 7, of which waited for: 6 -> 6; matrix products, arithmetic and copies ran while one was open for 5% -> 6% of each run, Pallas kernels for 0% -> 0%
where the time goes in v6:
time: 109 us; the launch traced here: 108 us
  waiting for transfers between devices  50.8 us (47%)
  starting transfers between devices  36.3 us (33%)
  blocking collectives  9.72 us (9%)
  other arithmetic  4.27 us (4%)
  local copies, waits for them, and re-layouts  2.93 us (3%)
  matrix products  2.08 us (2%)
  Pallas kernels  1.53 us (1%)
    all_to_all x1, waiting for transfers between devices, per_device(): lax.all_to_all(rows, 'expert', 0, 0, axis_index_groups=halves, tiled=True)  32.5 us
    all_to_all x1, starting transfers between devices, per_device(): lax.all_to_all(rows, 'expert', 0, 0, axis_index_groups=halves, tiled=True)  21 us
    all_gather x1, blocking collectives, per_device(): totals = lax.all_gather(squares, 'dp')  9.72 us
    ppermute x4, starting transfers between devices, shifted(): return lax.ppermute(block, 'pipe', route)  9.58 us
    ppermute x2, waiting for transfers between devices, shifted_to_partner(): return lax.ppermute(block, ('pipe', 'expert'), route)  9.55 us
    ppermute x4, waiting for transfers between devices, shifted(): return lax.ppermute(block, 'pipe', route)  8.83 us
    ppermute x2, starting transfers between devices, shifted_to_partner(): return lax.ppermute(block, ('pipe', 'expert'), route)  5.7 us
  transfers between devices with their start and end apart: 7, of which 6 were waited for; matrix products, arithmetic and copies ran while one was open for 6% of the time, Pallas kernels for 0%

profile of v6, /device:TPU:200, one launch (start us, length us, event | category | flops | bytes accessed | tf_op | source)
XLA Modules:
  0.0 108.5 jit_solution(1106420486010903303)
XLA Ops:
  0.6 0.0 copy-start
  0.7 1.2 %dynamic-slice_bitcast_fusion = (bf16[2,128,512]{2,1,0:T(8,128)(2,1)S(1)}, bf16[2,128,512]{2,1,0:T(8,128)(2,1)S(1)}) fusion(bf16[2,16,2,8,512]{4,3,2,1,0:T(8,128)(2,1)} %bitcast.55, s32[]{:T(128)S(6)} %select_n.79, s32[]{:T(128)S(6)} %select_n.78), kind=kLoop, calls=%fused_computation.30 | loop fusion | bytes 1048584 | tf_op jit(solution)/shard_map/reshape | solution.py:108
  1.9 0.4 copy-done
  2.3 0.4 convolution_convert_fusion.3
  2.7 1.9 %collective-permute-start = (bf16[128,1792]{1,0:T(8,128)(2,1)S(1)}, bf16[128,1792]{1,0:T(8,128)(2,1)S(1)}, u32[]{:S(2)}, u32[]{:S(2)}) collective-permute-start(bf16[128,1792]{1,0:T(8,128)(2,1)S(1)} %convolution_convert_fusion.3), channel_id=1, source_target_pairs={{0,132},{4,128},{8,140},{12,136},{16,148},{20,144},{24,156},{28,15... | collective-permute-start | bytes 1376264 | tf_op jit(solution)/shard_map/ppermute | solution.py:27
  4.6 0.4 convolution_convert_fusion.2
  5.1 2.7 %collective-permute-start.1 = (bf16[128,1792]{1,0:T(8,128)(2,1)S(1)}, bf16[128,1792]{1,0:T(8,128)(2,1)S(1)}, u32[]{:S(2)}, u32[]{:S(2)}) collective-permute-start(bf16[128,1792]{1,0:T(8,128)(2,1)S(1)} %convolution_convert_fusion.2), channel_id=1, source_target_pairs={{0,128},{128,256},{256,384},{384,512},{512,640},{640,768},{768,896... | collective-permute-start | bytes 1376264 | tf_op jit(solution)/shard_map/ppermute | solution.py:16
  7.8 0.4 convolution_convert_fusion.1
  8.2 3.8 %collective-permute-start.2 = (bf16[128,1792]{1,0:T(8,128)(2,1)S(1)}, bf16[128,1792]{1,0:T(8,128)(2,1)S(1)}, u32[]{:S(2)}, u32[]{:S(2)}) collective-permute-start(bf16[128,1792]{1,0:T(8,128)(2,1)S(1)} %convolution_convert_fusion.1), channel_id=1, source_target_pairs={{128,4},{132,0},{136,12},{140,8},{144,20},{148,16},{152,28},{156,2... | collective-permute-start | bytes 1376264 | tf_op jit(solution)/shard_map/ppermute | solution.py:27
  12.0 0.4 convolution_convert_fusion
  12.4 2.6 %collective-permute-start.3 = (bf16[128,1792]{1,0:T(8,128)(2,1)S(1)}, bf16[128,1792]{1,0:T(8,128)(2,1)S(1)}, u32[]{:S(2)}, u32[]{:S(2)}) collective-permute-start(bf16[128,1792]{1,0:T(8,128)(2,1)S(1)} %convolution_convert_fusion), channel_id=1, source_target_pairs={{128,0},{256,128},{384,256},{512,384},{640,512},{768,640},{896,768... | collective-permute-start | bytes 1376264 | tf_op jit(solution)/shard_map/ppermute | solution.py:16
  15.0 2.4 %collective-permute-done = bf16[128,1792]{1,0:T(8,128)(2,1)S(1)} collective-permute-done((bf16[128,1792]{1,0:T(8,128)(2,1)S(1)}, bf16[128,1792]{1,0:T(8,128)(2,1)S(1)}, u32[]{:S(2)}, u32[]{:S(2)}) %collective-permute-start) | collective-permute-done | bytes 458784 | tf_op jit(solution)/shard_map/ppermute | solution.py:27
  17.4 1.6 %collective-permute-done.1 = bf16[128,1792]{1,0:T(8,128)(2,1)S(1)} collective-permute-done((bf16[128,1792]{1,0:T(8,128)(2,1)S(1)}, bf16[128,1792]{1,0:T(8,128)(2,1)S(1)}, u32[]{:S(2)}, u32[]{:S(2)}) %collective-permute-start.1) | collective-permute-done | bytes 458784 | tf_op jit(solution)/shard_map/ppermute | solution.py:16
  19.1 0.1 fusion.12
  19.2 1.0 pad_maximum_fusion
  20.1 0.0 copy-start.2
  20.1 0.0 copy-start.3
  20.2 0.0 copy-start.1
  20.2 7.1 %collective-permute-done.2 = bf16[128,1792]{1,0:T(8,128)(2,1)S(1)} collective-permute-done((bf16[128,1792]{1,0:T(8,128)(2,1)S(1)}, bf16[128,1792]{1,0:T(8,128)(2,1)S(1)}, u32[]{:S(2)}, u32[]{:S(2)}) %collective-permute-start.2) | collective-permute-done | bytes 458784 | tf_op jit(solution)/shard_map/ppermute | solution.py:27
  27.3 0.0 collective-permute-done.3
  27.3 0.9 fusion.14
  28.2 21.0 %all-to-all-start = ((bf16[16,2,8,1792]{3,2,1,0:T(8,128)(2,1)}), bf16[16,2,8,1792]{3,2,1,0:T(8,128)(2,1)S(1)}, u32[]{:S(2)}, u32[]{:S(2)}) async-start(bf16[16,2,8,1792]{3,2,1,0:T(8,128)(2,1)} %fusion.14), calls=%async_computation | async-start | bytes 1835008 | tf_op jit(solution)/shard_map/all_to_all | solution.py:125
  49.1 0.0 copy-done.2
  49.2 0.1 copy.25
  49.2 0.1 copy.27
  49.3 0.0 copy-done.3
  49.3 0.1 copy.26
  49.4 0.1 copy.28
  49.5 0.4 compare_reduce_fusion
  49.9 0.4 fusion.11
  50.3 0.2 subtract_convert_fusion
  50.5 0.0 copy-done.1
  50.6 0.7 pad_maximum_fusion.2
  51.3 2.1 %collective-permute-start.5 = (bf16[64,2304]{1,0:T(8,128)(2,1)}, bf16[64,2304]{1,0:T(8,128)(2,1)S(1)}, u32[]{:S(2)}, u32[]{:S(2)}) collective-permute-start(bf16[64,2304]{1,0:T(8,128)(2,1)} %pad_maximum_fusion.2), channel_id=1, source_target_pairs={{128,0},{256,128},{384,256},{512,384},{640,512},{768,640},{896,768... | collective-permute-start | bytes 884744 | tf_op jit(solution)/shard_map/ppermute | solution.py:16
  53.5 0.2 subtract_convert_fusion.1
  53.7 0.7 pad_maximum_fusion.1
  54.4 2.2 %collective-permute-start.4 = (bf16[64,2304]{1,0:T(8,128)(2,1)}, bf16[64,2304]{1,0:T(8,128)(2,1)S(1)}, u32[]{:S(2)}, u32[]{:S(2)}) collective-permute-start(bf16[64,2304]{1,0:T(8,128)(2,1)} %pad_maximum_fusion.1), channel_id=1, source_target_pairs={{0,128},{128,256},{256,384},{384,512},{512,640},{640,768},{768,896... | collective-permute-start | bytes 884744 | tf_op jit(solution)/shard_map/ppermute | solution.py:16
  56.6 0.9 constant_dynamic-slice_fusion.1
  57.6 4.9 %collective-permute-done.5.side1_ref = bf16[64,2304]{1,0:T(8,128)(2,1)S(1)} collective-permute-done((bf16[64,2304]{1,0:T(8,128)(2,1)}, bf16[64,2304]{1,0:T(8,128)(2,1)S(1)}, u32[]{:S(2)}, u32[]{:S(2)}) %collective-permute-start.5) | collective-permute-done | bytes 294944 | tf_op jit(solution)/shard_map/ppermute | solution.py:16
  62.5 2.3 %collective-permute-done.4.side0_ref = bf16[64,2304]{1,0:T(8,128)(2,1)S(1)} collective-permute-done((bf16[64,2304]{1,0:T(8,128)(2,1)}, bf16[64,2304]{1,0:T(8,128)(2,1)S(1)}, u32[]{:S(2)}, u32[]{:S(2)}) %collective-permute-start.4) | collective-permute-done | bytes 294944 | tf_op jit(solution)/shard_map/ppermute | solution.py:16
  64.8 32.5 %all-to-all-done = bf16[16,2,8,1792]{3,2,1,0:T(8,128)(2,1)S(1)} async-done(((bf16[16,2,8,1792]{3,2,1,0:T(8,128)(2,1)}), bf16[16,2,8,1792]{3,2,1,0:T(8,128)(2,1)S(1)}, u32[]{:S(2)}, u32[]{:S(2)}) %all-to-all-start) | async-done | bytes 917536 | tf_op jit(solution)/shard_map/all_to_all | solution.py:125
  97.2 0.5 shard_map.77
  97.7 9.7 %all-gather.1.totals_ref = f32[4,2,64]{2,1,0:T(2,128)S(1)} all-gather(f32[1,2,64]{2,1,0:T(2,128)S(1)} %bitcast.54), channel_id=2, replica_groups=mesh['pipe'=8,'expert'=32,'dp'=4] {'dp'}, dimensions={0}, use_global_device_ids=true | all-gather | bytes 2560 | tf_op jit(solution)/shard_map/all_gather | solution.py:134
  107.5 1.0 shard_map.78
  (8 shorter events, 0.1 us)
Async XLA Ops:
  0.6 1.7 %copy-start = (bf16[1,512,1792]{2,1,0:T(8,128)(2,1)S(1)}, bf16[1,512,1792]{2,1,0:T(8,128)(2,1)}, u32[]{:S(2)}) copy-start(bf16[1,512,1792]{2,1,0:T(8,128)(2,1)} %param.10) | copy-start | bytes 5505028
  2.7 14.7 %collective-permute-start = (bf16[128,1792]{1,0:T(8,128)(2,1)S(1)}, bf16[128,1792]{1,0:T(8,128)(2,1)S(1)}, u32[]{:S(2)}, u32[]{:S(2)}) collective-permute-start(bf16[128,1792]{1,0:T(8,128)(2,1)S(1)} %convolution_convert_fusion.3), channel_id=1, source_target_pairs={{0,132},{4,128},{8,140},{12,136},{16,148},{20,144},{24,156},{28,15... | collective-permute-start | bytes 1376264 | tf_op jit(solution)/shard_map/ppermute | solution.py:27
  5.1 14.0 %collective-permute-start.1 = (bf16[128,1792]{1,0:T(8,128)(2,1)S(1)}, bf16[128,1792]{1,0:T(8,128)(2,1)S(1)}, u32[]{:S(2)}, u32[]{:S(2)}) collective-permute-start(bf16[128,1792]{1,0:T(8,128)(2,1)S(1)} %convolution_convert_fusion.2), channel_id=1, source_target_pairs={{0,128},{128,256},{256,384},{384,512},{512,640},{640,768},{768,896... | collective-permute-start | bytes 1376264 | tf_op jit(solution)/shard_map/ppermute | solution.py:16
  8.2 19.1 %collective-permute-start.2 = (bf16[128,1792]{1,0:T(8,128)(2,1)S(1)}, bf16[128,1792]{1,0:T(8,128)(2,1)S(1)}, u32[]{:S(2)}, u32[]{:S(2)}) collective-permute-start(bf16[128,1792]{1,0:T(8,128)(2,1)S(1)} %convolution_convert_fusion.1), channel_id=1, source_target_pairs={{128,4},{132,0},{136,12},{140,8},{144,20},{148,16},{152,28},{156,2... | collective-permute-start | bytes 1376264 | tf_op jit(solution)/shard_map/ppermute | solution.py:27
  12.4 14.9 %collective-permute-start.3 = (bf16[128,1792]{1,0:T(8,128)(2,1)S(1)}, bf16[128,1792]{1,0:T(8,128)(2,1)S(1)}, u32[]{:S(2)}, u32[]{:S(2)}) collective-permute-start(bf16[128,1792]{1,0:T(8,128)(2,1)S(1)} %convolution_convert_fusion), channel_id=1, source_target_pairs={{128,0},{256,128},{384,256},{512,384},{640,512},{768,640},{896,768... | collective-permute-start | bytes 1376264 | tf_op jit(solution)/shard_map/ppermute | solution.py:16
  20.1 29.0 %copy-start.2 = (s32[1,2,64,8]{2,3,1,0:T(8,128)S(1)}, s32[1,2,64,8]{2,3,1,0:T(8,128)}, u32[]{:S(2)}) copy-start(s32[1,2,64,8]{2,3,1,0:T(8,128)} %param.7) | copy-start | bytes 12292
  20.1 29.2 %copy-start.3 = (f32[1,2,64,8]{2,3,1,0:T(8,128)S(1)}, f32[1,2,64,8]{2,3,1,0:T(8,128)}, u32[]{:S(2)}) copy-start(f32[1,2,64,8]{2,3,1,0:T(8,128)} %param.8) | copy-start | bytes 12292
  20.2 30.4 %copy-start.1 = (bf16[1,2,64,1792]{3,2,1,0:T(8,128)(2,1)S(1)}, bf16[1,2,64,1792]{3,2,1,0:T(8,128)(2,1)}, u32[]{:S(2)}) copy-start(bf16[1,2,64,1792]{3,2,1,0:T(8,128)(2,1)} %param.6) | copy-start | bytes 1376260
  28.2 69.1 %all-to-all-start = ((bf16[16,2,8,1792]{3,2,1,0:T(8,128)(2,1)}), bf16[16,2,8,1792]{3,2,1,0:T(8,128)(2,1)S(1)}, u32[]{:S(2)}, u32[]{:S(2)}) async-start(bf16[16,2,8,1792]{3,2,1,0:T(8,128)(2,1)} %fusion.14), calls=%async_computation | async-start | bytes 1835008 | tf_op jit(solution)/shard_map/all_to_all | solution.py:125
  51.3 11.1 %collective-permute-start.5 = (bf16[64,2304]{1,0:T(8,128)(2,1)}, bf16[64,2304]{1,0:T(8,128)(2,1)S(1)}, u32[]{:S(2)}, u32[]{:S(2)}) collective-permute-start(bf16[64,2304]{1,0:T(8,128)(2,1)} %pad_maximum_fusion.2), channel_id=1, source_target_pairs={{128,0},{256,128},{384,256},{512,384},{640,512},{768,640},{896,768... | collective-permute-start | bytes 884744 | tf_op jit(solution)/shard_map/ppermute | solution.py:16
  54.4 10.3 %collective-permute-start.4 = (bf16[64,2304]{1,0:T(8,128)(2,1)}, bf16[64,2304]{1,0:T(8,128)(2,1)S(1)}, u32[]{:S(2)}, u32[]{:S(2)}) collective-permute-start(bf16[64,2304]{1,0:T(8,128)(2,1)} %pad_maximum_fusion.1), channel_id=1, source_target_pairs={{0,128},{128,256},{256,384},{384,512},{512,640},{640,768},{768,896... | collective-permute-start | bytes 884744 | tf_op jit(solution)/shard_map/ppermute | solution.py:16

commit v7 on v6

--- a/solution.py
+++ b/solution.py
@@ -113,7 +113,7 @@
         return jnp.dot(rows, down_weight[0], preferred_element_type=jnp.float32).astype(jnp.bfloat16)
 
     rows = None
-    for m, distance in enumerate((1, -1)):
+    for m, distance in ((1, -1), (0, 1)):
         theirs = shifted_to_partner(project(sent[m]), distance)
         own = shifted(project(kept[m]), distance)
         total = (theirs.astype(jnp.float32) + own.astype(jnp.float32)).astype(jnp.bfloat16)

time: 109 us -> 109 us (level)
  the two profiles are of different devices: /device:TPU:200 before, /device:TPU:72 now
where the time goes in v7:
time: 109 us
  waiting for transfers between devices  50.4 us (46%)
  starting transfers between devices  36.9 us (34%)
  blocking collectives  9.73 us (9%)
  other arithmetic  4.28 us (4%)
  local copies, waits for them, and re-layouts  2.93 us (3%)
  matrix products  2.08 us (2%)
  Pallas kernels  1.52 us (1%)
    all_to_all x1, waiting for transfers between devices, per_device(): lax.all_to_all(rows, 'expert', 0, 0, axis_index_groups=halves, tiled=True)  34.7 us
    ppermute x4, starting transfers between devices, shifted(): return lax.ppermute(block, 'pipe', route)  21.1 us
    all_to_all x1, starting transfers between devices, per_device(): lax.all_to_all(rows, 'expert', 0, 0, axis_index_groups=halves, tiled=True)  11.9 us
    all_gather x1, blocking collectives, per_device(): totals = lax.all_gather(squares, 'dp')  9.73 us
    ppermute x2, waiting for transfers between devices, shifted_to_partner(): return lax.ppermute(block, ('pipe', 'expert'), route)  8.19 us
    ppermute x4, waiting for transfers between devices, shifted(): return lax.ppermute(block, 'pipe', route)  7.5 us
    ppermute x2, starting transfers between devices, shifted_to_partner(): return lax.ppermute(block, ('pipe', 'expert'), route)  3.84 us
  transfers between devices with their start and end apart: 7, of which 6 were waited for; matrix products, arithmetic and copies ran while one was open for 6% of the time, Pallas kernels for 0%

profile of v7, /device:TPU:72, one launch (start us, length us, event | category | flops | bytes accessed | tf_op | source)
XLA Modules:
  0.0 108.6 jit_solution(14115068505669671295)
XLA Ops:
  0.6 0.0 copy-start
  0.7 1.2 %dynamic-slice_bitcast_fusion = (bf16[2,128,512]{2,1,0:T(8,128)(2,1)S(1)}, bf16[2,128,512]{2,1,0:T(8,128)(2,1)S(1)}) fusion(bf16[2,16,2,8,512]{4,3,2,1,0:T(8,128)(2,1)} %bitcast.55, s32[]{:T(128)S(6)} %select_n.79, s32[]{:T(128)S(6)} %select_n.78), kind=kLoop, calls=%fused_computation.30 | loop fusion | bytes 1048584 | tf_op jit(solution)/shard_map/reshape | solution.py:108
  1.9 0.4 copy-done
  2.3 0.4 convolution_convert_fusion.3
  2.7 1.9 %collective-permute-start = (bf16[128,1792]{1,0:T(8,128)(2,1)S(1)}, bf16[128,1792]{1,0:T(8,128)(2,1)S(1)}, u32[]{:S(2)}, u32[]{:S(2)}) collective-permute-start(bf16[128,1792]{1,0:T(8,128)(2,1)S(1)} %convolution_convert_fusion.3), channel_id=1, source_target_pairs={{128,4},{132,0},{136,12},{140,8},{144,20},{148,16},{152,28},{156,2... | collective-permute-start | bytes 1376264 | tf_op jit(solution)/shard_map/ppermute | solution.py:27
  4.6 0.4 convolution_convert_fusion.2
  5.1 14.4 %collective-permute-start.1 = (bf16[128,1792]{1,0:T(8,128)(2,1)S(1)}, bf16[128,1792]{1,0:T(8,128)(2,1)S(1)}, u32[]{:S(2)}, u32[]{:S(2)}) collective-permute-start(bf16[128,1792]{1,0:T(8,128)(2,1)S(1)} %convolution_convert_fusion.2), channel_id=1, source_target_pairs={{128,0},{256,128},{384,256},{512,384},{640,512},{768,640},{896,768... | collective-permute-start | bytes 1376264 | tf_op jit(solution)/shard_map/ppermute | solution.py:16
  19.4 0.4 convolution_convert_fusion.1
  19.9 1.9 %collective-permute-start.2 = (bf16[128,1792]{1,0:T(8,128)(2,1)S(1)}, bf16[128,1792]{1,0:T(8,128)(2,1)S(1)}, u32[]{:S(2)}, u32[]{:S(2)}) collective-permute-start(bf16[128,1792]{1,0:T(8,128)(2,1)S(1)} %convolution_convert_fusion.1), channel_id=1, source_target_pairs={{0,132},{4,128},{8,140},{12,136},{16,148},{20,144},{24,156},{28,15... | collective-permute-start | bytes 1376264 | tf_op jit(solution)/shard_map/ppermute | solution.py:27
  21.8 0.4 convolution_convert_fusion
  22.2 1.9 %collective-permute-start.3 = (bf16[128,1792]{1,0:T(8,128)(2,1)S(1)}, bf16[128,1792]{1,0:T(8,128)(2,1)S(1)}, u32[]{:S(2)}, u32[]{:S(2)}) collective-permute-start(bf16[128,1792]{1,0:T(8,128)(2,1)S(1)} %convolution_convert_fusion), channel_id=1, source_target_pairs={{0,128},{128,256},{256,384},{384,512},{512,640},{640,768},{768,896... | collective-permute-start | bytes 1376264 | tf_op jit(solution)/shard_map/ppermute | solution.py:16
  24.2 0.0 collective-permute-done
  24.2 1.3 %collective-permute-done.1 = bf16[128,1792]{1,0:T(8,128)(2,1)S(1)} collective-permute-done((bf16[128,1792]{1,0:T(8,128)(2,1)S(1)}, bf16[128,1792]{1,0:T(8,128)(2,1)S(1)}, u32[]{:S(2)}, u32[]{:S(2)}) %collective-permute-start.1) | collective-permute-done | bytes 458784 | tf_op jit(solution)/shard_map/ppermute | solution.py:16
  25.4 0.1 fusion.12
  25.5 1.0 pad_maximum_fusion
  26.5 0.0 copy-start.2
  26.5 0.0 copy-start.3
  26.5 0.0 copy-start.1
  26.5 8.2 %collective-permute-done.2 = bf16[128,1792]{1,0:T(8,128)(2,1)S(1)} collective-permute-done((bf16[128,1792]{1,0:T(8,128)(2,1)S(1)}, bf16[128,1792]{1,0:T(8,128)(2,1)S(1)}, u32[]{:S(2)}, u32[]{:S(2)}) %collective-permute-start.2) | collective-permute-done | bytes 458784 | tf_op jit(solution)/shard_map/ppermute | solution.py:27
  34.7 1.5 %collective-permute-done.3 = bf16[128,1792]{1,0:T(8,128)(2,1)S(1)} collective-permute-done((bf16[128,1792]{1,0:T(8,128)(2,1)S(1)}, bf16[128,1792]{1,0:T(8,128)(2,1)S(1)}, u32[]{:S(2)}, u32[]{:S(2)}) %collective-permute-start.3) | collective-permute-done | bytes 458784 | tf_op jit(solution)/shard_map/ppermute | solution.py:16
  36.2 0.9 fusion.14
  37.1 11.9 %all-to-all-start = ((bf16[16,2,8,1792]{3,2,1,0:T(8,128)(2,1)}), bf16[16,2,8,1792]{3,2,1,0:T(8,128)(2,1)S(1)}, u32[]{:S(2)}, u32[]{:S(2)}) async-start(bf16[16,2,8,1792]{3,2,1,0:T(8,128)(2,1)} %fusion.14), calls=%async_computation | async-start | bytes 1835008 | tf_op jit(solution)/shard_map/all_to_all | solution.py:125
  49.0 0.0 copy-done.2
  49.1 0.1 copy.25
  49.1 0.1 copy.27
  49.2 0.0 copy-done.3
  49.2 0.1 copy.26
  49.3 0.1 copy.28
  49.4 0.4 compare_reduce_fusion
  49.8 0.4 fusion.11
  50.2 0.2 subtract_convert_fusion
  50.4 0.0 copy-done.1
  50.5 0.7 pad_maximum_fusion.2
  51.2 1.9 %collective-permute-start.5 = (bf16[64,2304]{1,0:T(8,128)(2,1)}, bf16[64,2304]{1,0:T(8,128)(2,1)S(1)}, u32[]{:S(2)}, u32[]{:S(2)}) collective-permute-start(bf16[64,2304]{1,0:T(8,128)(2,1)} %pad_maximum_fusion.2), channel_id=1, source_target_pairs={{128,0},{256,128},{384,256},{512,384},{640,512},{768,640},{896,768... | collective-permute-start | bytes 884744 | tf_op jit(solution)/shard_map/ppermute | solution.py:16
  53.1 0.2 subtract_convert_fusion.1
  53.4 0.7 pad_maximum_fusion.1
  54.1 2.9 %collective-permute-start.4 = (bf16[64,2304]{1,0:T(8,128)(2,1)}, bf16[64,2304]{1,0:T(8,128)(2,1)S(1)}, u32[]{:S(2)}, u32[]{:S(2)}) collective-permute-start(bf16[64,2304]{1,0:T(8,128)(2,1)} %pad_maximum_fusion.1), channel_id=1, source_target_pairs={{0,128},{128,256},{256,384},{384,512},{512,640},{640,768},{768,896... | collective-permute-start | bytes 884744 | tf_op jit(solution)/shard_map/ppermute | solution.py:16
  57.0 0.9 constant_dynamic-slice_fusion.1
  57.9 0.5 collective-permute-done.5.side1_ref
  58.5 4.3 %collective-permute-done.4.side0_ref = bf16[64,2304]{1,0:T(8,128)(2,1)S(1)} collective-permute-done((bf16[64,2304]{1,0:T(8,128)(2,1)}, bf16[64,2304]{1,0:T(8,128)(2,1)S(1)}, u32[]{:S(2)}, u32[]{:S(2)}) %collective-permute-start.4) | collective-permute-done | bytes 294944 | tf_op jit(solution)/shard_map/ppermute | solution.py:16
  62.7 34.7 %all-to-all-done = bf16[16,2,8,1792]{3,2,1,0:T(8,128)(2,1)S(1)} async-done(((bf16[16,2,8,1792]{3,2,1,0:T(8,128)(2,1)}), bf16[16,2,8,1792]{3,2,1,0:T(8,128)(2,1)S(1)}, u32[]{:S(2)}, u32[]{:S(2)}) %all-to-all-start) | async-done | bytes 917536 | tf_op jit(solution)/shard_map/all_to_all | solution.py:125
  97.4 0.5 shard_map.77
  97.9 9.7 %all-gather.1.totals_ref = f32[4,2,64]{2,1,0:T(2,128)S(1)} all-gather(f32[1,2,64]{2,1,0:T(2,128)S(1)} %bitcast.54), channel_id=2, replica_groups=mesh['pipe'=8,'expert'=32,'dp'=4] {'dp'}, dimensions={0}, use_global_device_ids=true | all-gather | bytes 2560 | tf_op jit(solution)/shard_map/all_gather | solution.py:134
  107.6 1.0 shard_map.78
  (8 shorter events, 0.1 us)
Async XLA Ops:
  0.6 1.7 %copy-start = (bf16[1,512,1792]{2,1,0:T(8,128)(2,1)S(1)}, bf16[1,512,1792]{2,1,0:T(8,128)(2,1)}, u32[]{:S(2)}) copy-start(bf16[1,512,1792]{2,1,0:T(8,128)(2,1)} %param.10) | copy-start | bytes 5505028
  2.7 21.4 %collective-permute-start = (bf16[128,1792]{1,0:T(8,128)(2,1)S(1)}, bf16[128,1792]{1,0:T(8,128)(2,1)S(1)}, u32[]{:S(2)}, u32[]{:S(2)}) collective-permute-start(bf16[128,1792]{1,0:T(8,128)(2,1)S(1)} %convolution_convert_fusion.3), channel_id=1, source_target_pairs={{128,4},{132,0},{136,12},{140,8},{144,20},{148,16},{152,28},{156,2... | collective-permute-start | bytes 1376264 | tf_op jit(solution)/shard_map/ppermute | solution.py:27
  5.1 20.4 %collective-permute-start.1 = (bf16[128,1792]{1,0:T(8,128)(2,1)S(1)}, bf16[128,1792]{1,0:T(8,128)(2,1)S(1)}, u32[]{:S(2)}, u32[]{:S(2)}) collective-permute-start(bf16[128,1792]{1,0:T(8,128)(2,1)S(1)} %convolution_convert_fusion.2), channel_id=1, source_target_pairs={{128,0},{256,128},{384,256},{512,384},{640,512},{768,640},{896,768... | collective-permute-start | bytes 1376264 | tf_op jit(solution)/shard_map/ppermute | solution.py:16
  19.9 14.8 %collective-permute-start.2 = (bf16[128,1792]{1,0:T(8,128)(2,1)S(1)}, bf16[128,1792]{1,0:T(8,128)(2,1)S(1)}, u32[]{:S(2)}, u32[]{:S(2)}) collective-permute-start(bf16[128,1792]{1,0:T(8,128)(2,1)S(1)} %convolution_convert_fusion.1), channel_id=1, source_target_pairs={{0,132},{4,128},{8,140},{12,136},{16,148},{20,144},{24,156},{28,15... | collective-permute-start | bytes 1376264 | tf_op jit(solution)/shard_map/ppermute | solution.py:27
  22.2 14.0 %collective-permute-start.3 = (bf16[128,1792]{1,0:T(8,128)(2,1)S(1)}, bf16[128,1792]{1,0:T(8,128)(2,1)S(1)}, u32[]{:S(2)}, u32[]{:S(2)}) collective-permute-start(bf16[128,1792]{1,0:T(8,128)(2,1)S(1)} %convolution_convert_fusion), channel_id=1, source_target_pairs={{0,128},{128,256},{256,384},{384,512},{512,640},{640,768},{768,896... | collective-permute-start | bytes 1376264 | tf_op jit(solution)/shard_map/ppermute | solution.py:16
  26.5 22.5 %copy-start.2 = (s32[1,2,64,8]{2,3,1,0:T(8,128)S(1)}, s32[1,2,64,8]{2,3,1,0:T(8,128)}, u32[]{:S(2)}) copy-start(s32[1,2,64,8]{2,3,1,0:T(8,128)} %param.7) | copy-start | bytes 12292
  26.5 22.7 %copy-start.3 = (f32[1,2,64,8]{2,3,1,0:T(8,128)S(1)}, f32[1,2,64,8]{2,3,1,0:T(8,128)}, u32[]{:S(2)}) copy-start(f32[1,2,64,8]{2,3,1,0:T(8,128)} %param.8) | copy-start | bytes 12292
  26.5 23.9 %copy-start.1 = (bf16[1,2,64,1792]{3,2,1,0:T(8,128)(2,1)S(1)}, bf16[1,2,64,1792]{3,2,1,0:T(8,128)(2,1)}, u32[]{:S(2)}) copy-start(bf16[1,2,64,1792]{3,2,1,0:T(8,128)(2,1)} %param.6) | copy-start | bytes 1376260
  37.1 60.3 %all-to-all-start = ((bf16[16,2,8,1792]{3,2,1,0:T(8,128)(2,1)}), bf16[16,2,8,1792]{3,2,1,0:T(8,128)(2,1)S(1)}, u32[]{:S(2)}, u32[]{:S(2)}) async-start(bf16[16,2,8,1792]{3,2,1,0:T(8,128)(2,1)} %fusion.14), calls=%async_computation | async-start | bytes 1835008 | tf_op jit(solution)/shard_map/all_to_all | solution.py:125
  51.2 7.2 %collective-permute-start.5 = (bf16[64,2304]{1,0:T(8,128)(2,1)}, bf16[64,2304]{1,0:T(8,128)(2,1)S(1)}, u32[]{:S(2)}, u32[]{:S(2)}) collective-permute-start(bf16[64,2304]{1,0:T(8,128)(2,1)} %pad_maximum_fusion.2), channel_id=1, source_target_pairs={{128,0},{256,128},{384,256},{512,384},{640,512},{768,640},{896,768... | collective-permute-start | bytes 884744 | tf_op jit(solution)/shard_map/ppermute | solution.py:16
  54.1 8.6 %collective-permute-start.4 = (bf16[64,2304]{1,0:T(8,128)(2,1)}, bf16[64,2304]{1,0:T(8,128)(2,1)S(1)}, u32[]{:S(2)}, u32[]{:S(2)}) collective-permute-start(bf16[64,2304]{1,0:T(8,128)(2,1)} %pad_maximum_fusion.1), channel_id=1, source_target_pairs={{0,128},{128,256},{256,384},{384,512},{512,640},{640,768},{768,896... | collective-permute-start | bytes 884744 | tf_op jit(solution)/shard_map/ppermute | solution.py:16
